TPU v7x, 32 devices: a whole 2x2x4 slice. The times are simulated.
32 devices in a mesh: ctx: 8 (over z, x), head: 2 (over core), grp: 2 (over y).
Axes of the slice: x: 2, y: 2, z: 4, core: 2. Of those that a mesh axis runs over, the one named last changes fastest.
Arguments:
- tokens: bfloat16 [2, 2048, 3072], P('grp', 'ctx', 'head'), may hold values from -6 to 6
- modulation: bfloat16 [2, 3, 3072], P('grp'), may hold values from -3 to 3
- w_qkv: bfloat16 [3072, 3, 512], P(('ctx', 'grp'), None, 'head'), may hold values from -0.09021098 to 0.09021098
- query_gain: float32 [128], replicated, may hold values from 1 to 6
- key_gain: float32 [128], replicated, may hold values from 1 to 6
- w_out: bfloat16 [512, 3072], P('head'), may hold values from -0.25 to 0.25
Outputs:
- branch: bfloat16 [2, 2048, 3072], P('grp', 'ctx', 'head')
All inputs are finite; a program needn't handle non-finite values.
Results may differ from a plain program's by a relative error of at most 0.02.
The roundings to bfloat16 on the way count: a program that leaves them out, or rounds other values in their place, can miss the bound.
Values may be sent and summed in bfloat16 or wider, within the bound.
No kernel may reach another device: no remote copies, remote signals or barrier semaphores. Data moves between devices by JAX's collectives and lax.ppermute only.
A program may use at most 64 MiB of HBM per device.

v0:
```python
import jax
import jax.numpy as jnp
from jax import lax
from jax.sharding import PartitionSpec as P

HDIM = 128


def norm_heads(values, gain):
    mean_square = jnp.mean(values * values, axis=-1, keepdims=True)
    return (values * lax.rsqrt(mean_square + 1e-06) * gain).astype(jnp.bfloat16)


def attend_all(queries):
    scaling = HDIM ** (-0.5)

    def block_update(state, block_keys, block_values):
        highest, totals, summed = state
        scores = (
            jnp.einsum("qhd,khd->hqk", queries, block_keys, preferred_element_type=jnp.float32)
            * scaling
        )
        newest = jnp.maximum(highest, jnp.max(scores, axis=-1))
        factor = jnp.exp(highest - newest)
        weights = jnp.exp(scores - newest[..., None])
        totals = totals * factor + jnp.sum(weights, axis=-1)
        update = jnp.einsum(
            "hqk,khd->hqd",
            weights.astype(jnp.bfloat16),
            block_values,
            preferred_element_type=jnp.float32,
        )
        return (newest, totals, summed * factor[..., None] + update)

    def fold_keys(state, pieces, begin):
        piece_keys, piece_values = pieces
        count = piece_keys.shape[0]
        blocked_keys = piece_keys.reshape(
            count // 512, 512, piece_keys.shape[1], piece_keys.shape[2]
        )
        blocked_values = piece_values.reshape(
            count // 512, 512, piece_values.shape[1], piece_values.shape[2]
        )

        def step_block(inner, pair):
            return (block_update(inner, pair[0], pair[1]), None)

        state, unused = lax.scan(step_block, state, (blocked_keys, blocked_values))
        return state

    return fold_keys


def body(tokens, modulation, w_qkv, query_gain, key_gain, w_out):
    local_tokens = tokens.shape[1]
    local_heads = w_qkv.shape[2] // HDIM
    whole = lax.all_gather(tokens[0], "head", axis=1, tiled=True)
    floats = whole.astype(jnp.float32)
    center = jnp.mean(floats, axis=-1, keepdims=True)
    spread = jnp.mean((floats - center) ** 2, axis=-1, keepdims=True)
    normed = (floats - center) * lax.rsqrt(spread + 1e-06)
    mods = modulation[0].astype(jnp.float32)
    modulated = (normed * (1.0 + mods[1]) + mods[0]).astype(jnp.bfloat16)
    weight_rows = w_qkv.reshape(w_qkv.shape[0], 3 * w_qkv.shape[2])
    columns = modulated
    qkv = jnp.dot(
        columns,
        lax.all_gather(weight_rows, ("ctx", "grp"), axis=0, tiled=True),
        preferred_element_type=jnp.float32,
    )
    qkv = qkv.reshape(local_tokens, 3, local_heads, HDIM)
    queries = norm_heads(qkv[:, 0], query_gain)
    keys = norm_heads(qkv[:, 1], key_gain)
    values = qkv[:, 2].astype(jnp.bfloat16)
    start_state = (
        jnp.full((local_heads, local_tokens), -1e30, jnp.float32),
        jnp.zeros((local_heads, local_tokens), jnp.float32),
        jnp.zeros((local_heads, local_tokens, HDIM), jnp.float32),
    )
    highest, totals, summed = attend_all(queries)(
        start_state,
        (
            lax.all_gather(keys, "ctx", axis=0, tiled=True),
            lax.all_gather(values, "ctx", axis=0, tiled=True),
        ),
        jnp.int32(0),
    )
    attended = (
        (summed / totals[..., None])
        .transpose(1, 0, 2)
        .reshape(local_tokens, local_heads * HDIM)
        .astype(jnp.bfloat16)
    )
    feature_count = tokens.shape[2]
    columns = w_out
    projected = (
        lax.psum_scatter(
            lax.dot_general(
                columns, attended, (((0,), (1,)), ((), ())), preferred_element_type=jnp.float32
            ).astype(jnp.bfloat16),
            "head",
            scatter_dimension=0,
            tiled=True,
        )
        .astype(jnp.float32)
        .T
    )
    gate = lax.dynamic_slice_in_dim(
        mods[2], lax.axis_index("head") * feature_count, feature_count, 0
    )
    return (gate * projected).astype(jnp.bfloat16)[None]


def solution(mesh):
    in_specs = (
        P("grp", "ctx", "head"),
        P("grp", None, None),
        P(("ctx", "grp"), None, "head"),
        P(),
        P(),
        P("head", None),
    )
    out_specs = P("grp", "ctx", "head")
    return jax.shard_map(body, mesh=mesh, in_specs=in_specs, out_specs=out_specs, check_vma=False)
```

profile of v0, /device:TPU:1, one launch (start us, length us, event | category | flops | bytes accessed | tf_op | source)
XLA Modules:
  0.0 223.3 jit_solution(3327035270233296278)
XLA Ops:
  6.5 0.0 copy-start
  6.5 0.0 all-gather.11.cloned.1.call-start
  6.5 0.7 all-gather.11.cloned.1.call-update
  7.3 0.0 all-gather.7.cloned.1.call-start
  7.3 1.7 copy.24
  9.0 0.0 all-gather.7.cloned.1.call-update
  9.0 0.0 all-gather.9.cloned.1.call-start
  9.1 0.7 convert_element_type.47
  9.8 0.8 fusion.30
  10.7 10.5 %all-gather.11.cloned.1.call-done = bf16[1,256,3072]{2,1,0:T(8,128)(2,1)} async-done(((bf16[1,256,1536]{2,1,0:T(8,128)(2,1)}), bf16[1,256,3072]{2,1,0:T(8,128)(2,1)}) %all-gather.11.cloned.1.call-update) | async-done | bytes 1572880 | tf_op jit(solution)/shard_map/all_gather | solution.py:57
  21.2 0.0 copy-start.1
  21.2 1.8 convert_reduce_fusion
  23.0 2.0 fusion.17
  25.0 79.4 %all-gather.7.cloned.1.call-done = bf16[3072,768]{1,0:T(8,128)(2,1)} async-done(((bf16[192,768]{1,0:T(8,128)(2,1)}), bf16[3072,768]{1,0:T(8,128)(2,1)}) %all-gather.7.cloned.1.call-update) | async-done | bytes 4718608 | tf_op jit(solution)/shard_map/all_gather | solution.py:68
  104.4 0.0 copy-done.1
  104.4 0.0 copy-start.2
  104.4 4.8 %fusion.21 = f32[256,768]{1,0:T(8,128)} fusion(bf16[3072,768]{1,0:T(8,128)(2,1)} %all-gather.7.cloned.1.call-done, bf16[1,256,3072]{2,1,0:T(8,128)(2,1)S(1)} %copy-done.1, f32[3072]{0:T(1024)S(1)} %bitcast.74, f32[3072]{0:T(1024)S(1)} %bitcast.73, f32[256]{0:T(256)S(1)} %add_rsqrt_fusion.2, f32[256]{0:T(256)S(1)} %broadcast_multiply_fusion), kind=kOutput, calls=%fused_computation.30 | convolution fusion | flops 1212678144 | bytes 7104512 | tf_op jit(solution)/shard_map/dot_general | solution.py:66
  109.2 0.0 copy-start.3
  109.2 1.5 reshape.61
  110.8 0.2 fusion.29
  111.0 0.1 multiply_reduce_fusion.1
  111.1 0.0 copy-done.2
  111.2 0.8 multiply_convert_fusion.2
  111.9 0.0 all-gather.9.cloned.1.call-update
  112.0 0.0 all-gather.13.cloned.1.call-start
  112.0 0.1 slice.33
  112.1 0.7 copy.36
  112.8 0.0 all-gather.13.cloned.1.call-update
  112.8 0.0 reduce-scatter.2.cloned.1.call-start
  112.9 0.1 multiply_reduce_fusion
  113.1 0.0 copy-done.3
  113.1 0.1 multiply_convert_fusion.1
  113.2 37.6 %all-gather.9.cloned.1.call-done = bf16[2048,2,128]{2,0,1:T(8,128)(2,1)} async-done(((bf16[256,2,128]{2,0,1:T(8,128)(2,1)}), bf16[2048,2,128]{2,0,1:T(8,128)(2,1)}) %all-gather.9.cloned.1.call-update) | async-done | bytes 1048592 | tf_op jit(solution)/shard_map/all_gather | solution.py:83
  150.8 41.0 %all-gather.13.cloned.1.call-done = bf16[2048,1,2,128]{3,0,2,1:T(8,128)(2,1)} async-done(((bf16[256,1,2,128]{3,0,2,1:T(8,128)(2,1)}), bf16[2048,1,2,128]{3,0,2,1:T(8,128)(2,1)}) %all-gather.13.cloned.1.call-update) | async-done | bytes 1048592 | tf_op jit(solution)/shard_map/all_gather | solution.py:84
  191.8 11.5 %while.15 = (s32[]{:T(128)}, f32[2,256]{1,0:T(2,128)S(1)}, f32[2,256]{1,0:T(2,128)S(1)}, f32[2,256,128]{2,1,0:T(8,128)S(1)}, bf16[4,512,2,128]{3,1,0,2:T(8,128)(...) while((s32[]{:T(128)}, f32[2,256]{1,0:T(2,128)S(1)}, ...), condition=%wide.region_7.8_spmd.clone, body=%wide.region_4.7_spmd.clone.sunk | while | flops 135989760 | bytes 4359273 | solution.py:48
  191.8 1.3 fusion.45
  193.1 0.2 fusion.47
  193.3 1.4 convolution_add_fusion.2
  194.7 1.3 fusion.45
  196.0 0.2 fusion.47
  196.1 1.4 convolution_add_fusion.2
  197.6 1.3 fusion.45
  198.8 0.2 fusion.47
  199.0 1.4 convolution_add_fusion.2
  200.4 1.3 fusion.45
  201.7 0.2 fusion.47
  201.9 1.4 convolution_add_fusion.2
  203.3 0.1 copy.17
  203.5 0.0 copy-done
  203.5 1.8 fusion.13
  205.2 0.0 reduce-scatter.2.cloned.1.call-update
  205.3 9.3 %reduce-scatter.2.cloned.1.call-done = bf16[1536,256]{0,1:T(8,128)(2,1)} async-done(((bf16[3072,256]{0,1:T(8,128)(2,1)}), bf16[1536,256]{0,1:T(8,128)(2,1)}) %reduce-scatter.2.cloned.1.call-update) | async-done | bytes 786448 | tf_op jit(solution)/shard_map/reduce_scatter | solution.py:97
  214.6 2.1 fusion.27
  (22 shorter events, 0.2 us)
Async XLA Ops:
  6.5 196.9 %copy-start = (bf16[256,3072]{1,0:T(8,128)(2,1)S(1)}, bf16[256,3072]{1,0:T(8,128)(2,1)}, u32[]{:S(2)}) copy-start(bf16[256,3072]{1,0:T(8,128)(2,1)} %param.13) | copy-start | bytes 4718596
  6.5 14.7 %all-gather.11.cloned.1.call-start = ((), (), s32[]{:S(2)}) async-start(), calls=%async_computation.4 | async-start | bytes 2359296 | tf_op jit(solution)/shard_map/all_gather | solution.py:57
  7.3 97.2 %all-gather.7.cloned.1.call-start = ((), (), s32[]{:S(2)}) async-start(), calls=%async_computation.1 | async-start | bytes 5013504 | tf_op jit(solution)/shard_map/all_gather | solution.py:68
  9.0 141.8 %all-gather.9.cloned.1.call-start = ((), (), s32[]{:S(2)}) async-start(), calls=%async_computation.2 | async-start | bytes 1179648 | tf_op jit(solution)/shard_map/all_gather | solution.py:83
  21.2 83.2 %copy-start.1 = (bf16[1,256,3072]{2,1,0:T(8,128)(2,1)S(1)}, bf16[1,256,3072]{2,1,0:T(8,128)(2,1)}, u32[]{:S(2)}) copy-start(bf16[1,256,3072]{2,1,0:T(8,128)(2,1)} %all-gather.11.cloned.1.call-done) | copy-start | bytes 4718596
  104.4 6.7 %copy-start.2 = (f32[128]{0:T(128)S(1)}, f32[128]{0:T(128)}, u32[]{:S(2)}) copy-start(f32[128]{0:T(128)} %param.12) | copy-start | bytes 1540
  109.2 3.8 %copy-start.3 = (f32[128]{0:T(128)S(1)}, f32[128]{0:T(128)}, u32[]{:S(2)}) copy-start(f32[128]{0:T(128)} %param.11) | copy-start | bytes 1540
  112.0 79.8 %all-gather.13.cloned.1.call-start = ((), (), s32[]{:S(2)}) async-start(), calls=%async_computation.5 | async-start | bytes 1179648 | tf_op jit(solution)/shard_map/all_gather | solution.py:84
  112.8 101.8 %reduce-scatter.2.cloned.1.call-start = ((), (), s32[]{:S(2)}) async-start(), calls=%async_computation.3 | async-start | bytes 2359296 | tf_op jit(solution)/shard_map/reduce_scatter | solution.py:97
Sparse Core Ops, SparseCore 0:
  8.9 12.2 all-gather.10
  24.0 80.3 all-gather.6
  112.1 38.6 all-gather.8
  152.8 38.9 all-gather.12
  205.4 9.1 reduce-scatter.1
where the time goes:
time: 224 us; the launch traced here: 223 us
  waiting for transfers between devices  179 us (80%)
  matrix products  17.1 us (8%)
  between operations  13.3 us (6%)
  other arithmetic  8.7 us (4%)
  local copies, waits for them, and re-layouts  5.2 us (2%)
    all_gather x1, waiting for transfers between devices, body(): lax.all_gather(weight_rows, ('ctx', 'grp'), axis=0, tiled=True)  79.4 us
    all_gather x1, waiting for transfers between devices, body(): lax.all_gather(values, 'ctx', axis=0, tiled=True)  41 us
    all_gather x1, waiting for transfers between devices, body(): lax.all_gather(keys, 'ctx', axis=0, tiled=True)  37.6 us
    all_gather x1, waiting for transfers between devices, body(): whole = lax.all_gather(tokens[0], 'head', axis=1, tiled=True)  10.5 us
    reduce_scatter x1, waiting for transfers between devices, body(): lax.psum_scatter(lax.dot_general(columns, attended, (((0,), (1,)), ((), (...  9.32 us
    dot_general x4, matrix products, block_update(): jnp.einsum('hqk,khd->hqd', weights.astype(jnp.bfloat16), block_values, pr...  5.5 us
    dot_general x4, matrix products, block_update(): jnp.einsum('qhd,khd->hqk', queries, block_keys, preferred_element_type=jn...  5.06 us
    dot_general x1, matrix products, body(): jnp.dot(columns, lax.all_gather(weight_rows, ('ctx', 'grp'), axis=0, tile...  4.81 us
  transfers between devices with their start and end apart: 5, of which 5 were waited for; matrix products, arithmetic and copies ran while one was open for 4% of the time, Pallas kernels for 0%

commit v1 on v0

v1 whole, which is shorter than its diff:
```python
import functools
import math

import jax
import jax.numpy as jnp
from jax import lax
from jax.experimental import pallas as pl
from jax.experimental.pallas import tpu as pltpu
from jax.sharding import PartitionSpec as P

HDIM = 128
PAIR = 2
VMEM_LIMIT = 40 * 1024 * 1024
VMEM_SPEC = pl.BlockSpec(memory_space=pltpu.VMEM)


def call(kernel, out_shape, scratch=()):
    return lambda *args: pl.pallas_call(
        kernel,
        out_shape=out_shape,
        in_specs=[VMEM_SPEC] * len(args),
        out_specs=jax.tree.map(lambda unused: VMEM_SPEC, out_shape),
        scratch_shapes=list(scratch),
        compiler_params=pltpu.CompilerParams(vmem_limit_bytes=VMEM_LIMIT),
    )(*args)


def swap(value, axes, sizes, flips):
    total = math.prod(sizes)
    perm = []
    for source in range(total):
        rest, target, weight = source, 0, 1
        for size, flip in zip(reversed(sizes), reversed(flips)):
            target += ((rest % size) ^ flip) * weight
            weight *= size
            rest //= size
        perm.append((source, target))
    return lax.ppermute(value, tuple(axes), perm)


def after(value, *others):
    return lax.optimization_barrier((value, others))[0] if others else value


def all_features(piece, n_head):
    return [piece] + [swap(piece, ["head"], [n_head], [j]) for j in range(1, n_head)]


def spread(piece, n_ctx):
    held = {0: piece}
    bit = n_ctx // PAIR // 2
    while bit:
        for far, one in list(held.items()):
            held[far ^ bit] = swap(one, ["ctx"], [n_ctx], [bit * PAIR])
        bit //= 2
    return [held[far] for far in range(n_ctx // PAIR)]


def norm_rows(pieces, mods_ref, out_ref):
    me = lax.axis_index("head")
    rows, width = pieces[0].shape
    total = width * len(pieces)
    step = 16
    places = [
        pl.ds(pl.multiple_of((me ^ j) * width, 128), width) for j in range(len(pieces))
    ]

    def block(i, unused):
        here = pl.ds(pl.multiple_of(i * step, step), step)
        floats = [piece[here, :].astype(jnp.float32) for piece in pieces]
        center = sum(jnp.sum(x, axis=-1, keepdims=True) for x in floats) / total
        floats = [x - center for x in floats]
        spread = sum(jnp.sum(x * x, axis=-1, keepdims=True) for x in floats) / total
        inverse = lax.rsqrt(spread + 1e-06)
        for x, place in zip(floats, places):
            shift = mods_ref[0:1, place].astype(jnp.float32)
            scale = 1.0 + mods_ref[1:2, place].astype(jnp.float32)
            out_ref[here, place] = (x * inverse * scale + shift).astype(jnp.bfloat16)
        return unused

    lax.fori_loop(0, rows // step, block, 0, unroll=4)


def norm_kernel(n_head, *refs):
    norm_rows(refs[:n_head], *refs[n_head:])


def project(tokens_ref, gains, weights, q_ref, kv_ref):
    out = jnp.dot(tokens_ref[...], weights[...], preferred_element_type=jnp.float32)
    for part, gain_ref in enumerate(gains):
        one = out[:, part * HDIM : (part + 1) * HDIM]
        mean_square = jnp.mean(one * one, axis=-1, keepdims=True)
        one = (one * lax.rsqrt(mean_square + 1e-06) * gain_ref[...]).astype(jnp.bfloat16)
        if part == 0:
            q_ref[...] = one
        else:
            kv_ref[:, :HDIM] = one
    kv_ref[:, HDIM:] = out[:, 2 * HDIM :].astype(jnp.bfloat16)


def first_qkv_kernel(places, n_grp, *refs):
    tokens_ref, qgain_ref, kgain_ref = refs[:3]
    chunks, (q_ref, kv_ref, weights) = refs[3:-3], refs[-3:]
    t = lax.axis_index("ctx")
    g = lax.axis_index("grp")
    rows = chunks[0].shape[0]
    for (far, near, fg), chunk in zip(places, chunks):
        owner = t ^ (far * PAIR + near)
        start = pl.multiple_of((owner * n_grp + (g ^ fg)) * rows, 16)
        weights[pl.ds(start, rows), :] = chunk[...]
    project(tokens_ref, (qgain_ref, kgain_ref), weights, q_ref, kv_ref)


def norm_qkv_kernel(n_head, *refs):
    pieces, (mods_ref, qgain_ref, kgain_ref, weights, q_ref, kv_ref, normed) = (
        refs[:n_head],
        refs[n_head:],
    )
    norm_rows(pieces, mods_ref, normed)
    project(normed, (qgain_ref, kgain_ref), weights, q_ref, kv_ref)


def attend_kernel(count, *refs):
    q_refs, pieces, out_refs = refs[:PAIR], refs[PAIR : PAIR + count], refs[PAIR + count :]
    step = 128
    factor = HDIM ** (-0.5) * math.log2(math.e)
    dims = (((1,), (1,)), ((), ()))
    for q_ref, out_ref in zip(q_refs, out_refs):
        for i in range(q_ref.shape[0] // step):
            here = slice(i * step, (i + 1) * step)
            query = q_ref[here, :]
            scores = [
                lax.dot_general(query, piece[:, :HDIM], dims, preferred_element_type=jnp.float32)
                for piece in pieces
            ]
            highest = functools.reduce(
                jnp.maximum, [jnp.max(s, axis=-1, keepdims=True) for s in scores]
            )
            total = jnp.zeros((step, 1), jnp.float32)
            mixed = jnp.zeros((step, HDIM), jnp.float32)
            for s, piece in zip(scores, pieces):
                weights = jnp.exp2((s - highest) * factor)
                total = total + jnp.sum(weights, axis=-1, keepdims=True)
                mixed = mixed + jnp.dot(
                    weights.astype(jnp.bfloat16),
                    piece[:, HDIM:],
                    preferred_element_type=jnp.float32,
                )
            out_ref[here, :] = (mixed / total).astype(jnp.bfloat16)


def out_kernel(n_head, *refs):
    heads = refs[: PAIR * n_head]
    w_refs = refs[PAIR * n_head : (PAIR + 1) * n_head]
    gate_ref, out_ref, att = refs[(PAIR + 1) * n_head :]
    c = lax.axis_index("head")
    p = lax.axis_index("ctx") % PAIR
    width = out_ref.shape[1]
    mine = pl.ds(pl.multiple_of(c * width, 128), width)
    projected = None
    for j in range(n_head):
        for a in range(PAIR):
            where = pl.ds(pl.multiple_of((p ^ a) * HDIM, HDIM), HDIM)
            att[j, :, where] = heads[j * PAIR + a][...]
        w_rows = w_refs[j][...] if j else w_refs[j][:, mine]
        partial = jnp.dot(att[j], w_rows, preferred_element_type=jnp.float32)
        partial = partial.astype(jnp.bfloat16).astype(jnp.float32)
        projected = partial if projected is None else projected + partial
    gate = gate_ref[2:3, mine].astype(jnp.float32)
    out_ref[...] = (gate * projected).astype(jnp.bfloat16)


def body(sizes, tokens, modulation, w_qkv, query_gain, key_gain, w_out):
    n_ctx, n_head, n_grp = sizes["ctx"], sizes["head"], sizes["grp"]
    t, c = lax.axis_index("ctx"), lax.axis_index("head")
    p = t % PAIR
    tokens, mods = tokens[0], modulation[0]
    count, width = tokens.shape
    rows = w_qkv.shape[0]

    far_count = n_ctx // PAIR
    mine = lax.dynamic_slice_in_dim(w_qkv, p * HDIM, HDIM, 2).reshape(rows, 3 * HDIM)
    given = lax.dynamic_slice_in_dim(w_qkv, (1 - p) * HDIM, HDIM, 2).reshape(rows, 3 * HDIM)
    other = swap(given, ["ctx"], [n_ctx], [1])
    wide = jax.ShapeDtypeStruct((count, width * n_head), jnp.bfloat16)
    own_normed = call(functools.partial(norm_kernel, n_head), wide)(
        *all_features(tokens, n_head), mods
    )

    rows_out = after(w_out, own_normed)
    blocks = [
        lax.dynamic_slice_in_dim(rows_out, (c ^ j) * width, width, 1) for j in range(1, n_head)
    ]
    outs = [swap(block, ["head"], [n_head], [j]) for j, block in enumerate(blocks, 1)]

    chunks, places = [], []
    held = [spread(mine, n_ctx), spread(other, n_ctx)]
    sent = []
    for far in range(far_count):
        for near in range(PAIR):
            piece = held[near][far]
            if len(sent) == 3:
                sent[1] += (own_normed, *blocks)
            if len(sent) >= 2:
                piece = after(piece, *sent[-2])
            if 0 < far < far_count - 1:
                piece = after(piece, held[near][far + 1])
            got = [swap(piece, ["grp"], [n_grp], [fg]) for fg in range(1, n_grp)]
            sent.append(tuple(got))
            for fg, chunk in enumerate([held[near][far]] + got):
                chunks.append(chunk)
                places.append((far, near, fg))
    first = (other, held[0][far_count // 2], held[0][1], *sent[0])
    neighbour = swap(after(tokens, *first), ["ctx"], [n_ctx], [1])
    neighbour = after(neighbour, *sent[-4], *sent[-3])

    piece_shape = jax.ShapeDtypeStruct((count, HDIM), jnp.bfloat16)
    pair_shape = jax.ShapeDtypeStruct((count, 2 * HDIM), jnp.bfloat16)
    gains = (query_gain[None], key_gain[None])
    own_queries, own_kv, weights = call(
        functools.partial(first_qkv_kernel, places, n_grp),
        (
            piece_shape,
            pair_shape,
            jax.ShapeDtypeStruct((rows * len(places), 3 * HDIM), jnp.bfloat16),
        ),
    )(own_normed, *gains, *chunks)
    other_queries, other_kv = call(
        functools.partial(norm_qkv_kernel, n_head),
        (piece_shape, pair_shape),
        [pltpu.VMEM(wide.shape, jnp.bfloat16)],
    )(*all_features(neighbour, n_head), mods, *gains, weights)

    gathered = spread(own_kv, n_ctx) + spread(other_kv, n_ctx)
    att_own, att_other = call(
        functools.partial(attend_kernel, len(gathered)), (piece_shape, piece_shape)
    )(own_queries, other_queries, *gathered)

    heads = []
    for j in range(n_head):
        for a in range(PAIR):
            piece = att_other if a else att_own
            if j or a:
                piece = swap(piece, ["ctx", "head"], [n_ctx, n_head], [a, j])
            heads.append(piece)
    branch = call(
        functools.partial(out_kernel, n_head),
        jax.ShapeDtypeStruct((count, width), jnp.bfloat16),
        [pltpu.VMEM((n_head, count, PAIR * HDIM), jnp.bfloat16)],
    )(*heads, w_out, *outs, mods)
    return branch[None]


def solution(mesh):
    in_specs = (
        P("grp", "ctx", "head"),
        P("grp", None, None),
        P(("ctx", "grp"), None, "head"),
        P(),
        P(),
        P("head", None),
    )
    out_specs = P("grp", "ctx", "head")
    return jax.shard_map(
        functools.partial(body, dict(mesh.shape)),
        mesh=mesh,
        in_specs=in_specs,
        out_specs=out_specs,
        check_vma=False,
    )
```

time: 224 us -> 80.9 us (0.36)
  waiting for transfers between devices: 179 us -> 39.2 us
  starting transfers between devices: 0.17 us -> 30.5 us
  matrix products: 17.1 us -> 0 us
  between operations: 13.3 us -> 0.11 us
  Pallas kernels: 0 us -> 8.87 us
  other arithmetic: 8.7 us -> 0 us
  local copies, waits for them, and re-layouts: 5.2 us -> 1.94 us
    all_gather x4 -> x0, waiting for transfers between devices: 169 us -> none  [the longest x1 79.4 us: body(): lax.all_gather(weight_rows, ('ctx', 'grp'), axis=0, tiled=True)]
    ppermute x0 -> x28, waiting for transfers between devices: none -> 39.2 us  [swap(): return lax.ppermute(value, tuple(axes), perm)]
    ppermute x0 -> x28, starting transfers between devices: none -> 30.5 us  [swap(): return lax.ppermute(value, tuple(axes), perm)]
    dot_general x10 -> x0, matrix products: 17.1 us -> none  [the longest x4 5.5 us: block_update(): jnp.einsum('hqk,khd->hqd', weights.astype(jnp.bfloat16), block_values, pr...]
    reduce_scatter x1 -> x0, waiting for transfers between devices: 9.32 us -> none  [body(): lax.psum_scatter(lax.dot_general(columns, attended, (((0,), (1,)), ((), (...]
    pallas_call x0 -> x5, Pallas kernels: none -> 8.87 us  [call(): pl.pallas_call(kernel, out_shape=out_shape, in_specs=[VMEM_SPEC] * len(ar...]
    reduce_sum x8 -> x0, other arithmetic: 4.71 us -> none  [the longest x1 1.96 us: body(): spread = jnp.mean((floats - center) ** 2, axis=-1, keepdims=True)]
    reshape x2, local copies, waits for them, and re-layouts: 3.23 us -> 0.05 us  [the longest x1 0.03 us: body(): lax.dynamic_slice_in_dim(w_qkv, p * HDIM, HDIM, 2).reshape(rows, 3 * HDIM)]
  transfers between devices with their start and end apart: 5 -> 28, of which waited for: 5 -> 17; matrix products, arithmetic and copies ran while one was open for 4% -> 1% of each run, Pallas kernels for 0% -> 9%
where the time goes in v1:
time: 80.9 us; the launch traced here: 80.7 us
  waiting for transfers between devices  39.2 us (48%)
  starting transfers between devices  30.5 us (38%)
  Pallas kernels  8.87 us (11%)
  local copies, waits for them, and re-layouts  1.94 us (2%)
    ppermute x28, waiting for transfers between devices, swap(): return lax.ppermute(value, tuple(axes), perm)  39.2 us
    ppermute x28, starting transfers between devices, swap(): return lax.ppermute(value, tuple(axes), perm)  30.5 us
    pallas_call x5, Pallas kernels, call(): pl.pallas_call(kernel, out_shape=out_shape, in_specs=[VMEM_SPEC] * len(ar...  8.87 us
    unnamed x13, local copies, waits for them, and re-layouts  1.83 us
  transfers between devices with their start and end apart: 28, of which 17 were waited for; matrix products, arithmetic and copies ran while one was open for 1% of the time, Pallas kernels for 9%

profile of v1, /device:TPU:1, one launch (start us, length us, event | category | flops | bytes accessed | tf_op | source)
XLA Modules:
  0.0 80.7 jit_solution(12636711055456546644)
XLA Ops:
  0.0 0.1 collective-permute-start
  0.1 1.1 %dynamic-slice_bitcast_fusion = (bf16[3,24,8,128]{3,2,1,0:T(8,128)(2,1)S(1)}, bf16[3,24,8,128]{3,2,1,0:T(8,128)(2,1)S(1)}) fusion(bf16[192,3,256]{2,0,1:T(8,128)(2,1)} %param.8, s32[]{:T(128)S(6)} %select_n.18, s32[]{:T(128)S(6)} %select_n.17), kind=kLoop, calls=%fused_computation.2 | loop fusion | bytes 589832
  1.2 2.7 %collective-permute-start.1 = (bf16[192,384]{1,0:T(8,128)(2,1)S(1)}, bf16[192,384]{1,0:T(8,128)(2,1)S(1)}, u32[]{:S(2)}, u32[]{:S(2)}) collective-permute-start(bf16[192,384]{1,0:T(8,128)(2,1)S(1)} %bitcast.18), channel_id=1, source_target_pairs={{0,1},{1,0},{2,3},{3,2},{4,5},{5,4},{6,7},{7,6},{8,9},{9,8},{10,11... | collective-permute-start | bytes 442376 | tf_op jit(solution)/shard_map/ppermute | solution.py:38
  3.9 1.3 %collective-permute-start.2 = (bf16[192,384]{1,0:T(8,128)(2,1)S(1)}, bf16[192,384]{1,0:T(8,128)(2,1)S(1)}, u32[]{:S(2)}, u32[]{:S(2)}) collective-permute-start(bf16[192,384]{1,0:T(8,128)(2,1)S(1)} %bitcast.29), channel_id=1, source_target_pairs={{0,4},{4,0},{8,12},{12,8},{16,20},{20,16},{24,28},{28,24},{1,5},{5... | collective-permute-start | bytes 442376 | tf_op jit(solution)/shard_map/ppermute | solution.py:38
  5.2 1.3 %collective-permute-start.4 = (bf16[192,384]{1,0:T(8,128)(2,1)S(1)}, bf16[192,384]{1,0:T(8,128)(2,1)S(1)}, u32[]{:S(2)}, u32[]{:S(2)}) collective-permute-start(bf16[192,384]{1,0:T(8,128)(2,1)S(1)} %bitcast.19), channel_id=1, source_target_pairs={{0,8},{4,12},{8,0},{12,4},{16,24},{20,28},{24,16},{28,20},{1,9},{5... | collective-permute-start | bytes 442376 | tf_op jit(solution)/shard_map/ppermute | solution.py:38
  6.5 2.3 %collective-permute-start.5 = (bf16[192,384]{1,0:T(8,128)(2,1)S(1)}, bf16[192,384]{1,0:T(8,128)(2,1)S(1)}, u32[]{:S(2)}, u32[]{:S(2)}) collective-permute-start(bf16[192,384]{1,0:T(8,128)(2,1)S(1)} %bitcast.20), channel_id=1, source_target_pairs={{0,16},{4,20},{8,24},{12,28},{16,0},{20,4},{24,8},{28,12},{1,17},{... | collective-permute-start | bytes 442376 | tf_op jit(solution)/shard_map/ppermute | solution.py:38
  8.8 0.0 collective-permute-done.1.refs_4_
  8.8 0.3 collective-permute-done.2.refs_5_
  9.1 0.9 %collective-permute-done.4.refs_7_ = bf16[192,384]{1,0:T(8,128)(2,1)S(1)} collective-permute-done((bf16[192,384]{1,0:T(8,128)(2,1)S(1)}, bf16[192,384]{1,0:T(8,128)(2,1)S(1)}, u32[]{:S(2)}, u32[]{:S(2)}) %collective-permute-start.4) | collective-permute-done | bytes 147488 | tf_op jit(solution)/shard_map/ppermute | solution.py:38
  9.9 2.6 %collective-permute-done.5.refs_11_ = bf16[192,384]{1,0:T(8,128)(2,1)S(1)} collective-permute-done((bf16[192,384]{1,0:T(8,128)(2,1)S(1)}, bf16[192,384]{1,0:T(8,128)(2,1)S(1)}, u32[]{:S(2)}, u32[]{:S(2)}) %collective-permute-start.5) | collective-permute-done | bytes 147488 | tf_op jit(solution)/shard_map/ppermute | solution.py:38
  12.5 0.3 collective-permute-start.16
  12.8 0.2 collective-permute-start.6
  13.0 1.2 %collective-permute-start.3 = (bf16[192,384]{1,0:T(8,128)(2,1)S(1)}, bf16[192,384]{1,0:T(8,128)(2,1)S(1)}, u32[]{:S(2)}, u32[]{:S(2)}) collective-permute-start(bf16[192,384]{1,0:T(8,128)(2,1)S(1)} %collective-permute-done.2.refs_5_), channel_id=1, source_target_pairs={{0,1},{1,0},{2,3},{3,2},{4,5},{5,4},{6,7},{7,6},{8,9},{9,8},{10,11... | collective-permute-start | bytes 442376 | tf_op jit(solution)/shard_map/ppermute | solution.py:38
  14.2 2.9 %collective-permute-start.7 = (bf16[192,384]{1,0:T(8,128)(2,1)S(1)}, bf16[192,384]{1,0:T(8,128)(2,1)S(1)}, u32[]{:S(2)}, u32[]{:S(2)}) collective-permute-start(bf16[192,384]{1,0:T(8,128)(2,1)S(1)} %collective-permute-done.2.refs_5_), channel_id=1, source_target_pairs={{0,8},{4,12},{8,0},{12,4},{16,24},{20,28},{24,16},{28,20},{1,9},{5... | collective-permute-start | bytes 442376 | tf_op jit(solution)/shard_map/ppermute | solution.py:38
  17.2 0.0 collective-permute-done.refs_1_
  17.2 2.3 %collective-permute-start.8 = (bf16[192,384]{1,0:T(8,128)(2,1)S(1)}, bf16[192,384]{1,0:T(8,128)(2,1)S(1)}, u32[]{:S(2)}, u32[]{:S(2)}) collective-permute-start(bf16[192,384]{1,0:T(8,128)(2,1)S(1)} %collective-permute-done.2.refs_5_), channel_id=1, source_target_pairs={{0,16},{4,20},{8,24},{12,28},{16,0},{20,4},{24,8},{28,12},{1,17},{... | collective-permute-start | bytes 442376 | tf_op jit(solution)/shard_map/ppermute | solution.py:38
  19.4 0.7 copy-done.2
  20.2 1.4 %shard_map.64.refs_0_ = bf16[256,3072]{1,0:T(8,128)(2,1)S(1)} custom-call(bf16[256,1536]{1,0:T(8,128)(2,1)S(1)} %bitcast.17, bf16[256,1536]{1,0:T(8,128)(2,1)S(1)} %collective-permute-done.refs_1_, bf16[3,3072]{1,0:T(4,128)(2,1)S(1)} %bitcast.22), custom_call_target="tpu_custom_call" | custom-call | tf_op jit(solution)/shard_map/pallas_call | solution.py:18
  21.6 0.0 copy-done
  21.6 0.0 copy-start.4
  21.6 0.0 copy-start.5
  21.6 0.1 constant_dynamic-slice_fusion
  21.7 0.0 collective-permute-done.3.refs_6_
  21.7 0.7 collective-permute-start.10
  22.4 0.0 collective-permute-done.7.refs_9_
  22.4 1.1 %collective-permute-done.8.refs_13_ = bf16[192,384]{1,0:T(8,128)(2,1)S(1)} collective-permute-done((bf16[192,384]{1,0:T(8,128)(2,1)S(1)}, bf16[192,384]{1,0:T(8,128)(2,1)S(1)}, u32[]{:S(2)}, u32[]{:S(2)}) %collective-permute-start.8) | collective-permute-done | bytes 147488 | tf_op jit(solution)/shard_map/ppermute | solution.py:38
  23.5 0.2 collective-permute-start.9
  23.7 0.6 collective-permute-start.12
  24.3 0.0 collective-permute-done.6.refs_8_
  24.3 3.3 %collective-permute-done.10.refs_15_ = bf16[192,384]{1,0:T(8,128)(2,1)S(1)} collective-permute-done((bf16[192,384]{1,0:T(8,128)(2,1)S(1)}, bf16[192,384]{1,0:T(8,128)(2,1)S(1)}, u32[]{:S(2)}, u32[]{:S(2)}) %collective-permute-start.10) | collective-permute-done | bytes 147488 | tf_op jit(solution)/shard_map/ppermute | solution.py:38
  27.6 0.2 collective-permute-start.11
  27.8 0.0 collective-permute-done.9.refs_10_
  27.8 2.5 %collective-permute-done.12.refs_17_ = bf16[192,384]{1,0:T(8,128)(2,1)S(1)} collective-permute-done((bf16[192,384]{1,0:T(8,128)(2,1)S(1)}, bf16[192,384]{1,0:T(8,128)(2,1)S(1)}, u32[]{:S(2)}, u32[]{:S(2)}) %collective-permute-start.12) | collective-permute-done | bytes 147488 | tf_op jit(solution)/shard_map/ppermute | solution.py:38
  30.4 0.2 collective-permute-start.13
  30.6 2.5 %collective-permute-done.11.refs_12_ = bf16[192,384]{1,0:T(8,128)(2,1)S(1)} collective-permute-done((bf16[192,384]{1,0:T(8,128)(2,1)S(1)}, bf16[192,384]{1,0:T(8,128)(2,1)S(1)}, u32[]{:S(2)}, u32[]{:S(2)}) %collective-permute-start.11) | collective-permute-done | bytes 147488 | tf_op jit(solution)/shard_map/ppermute | solution.py:38
  33.1 0.0 collective-permute-done.16.refs_0_
  33.1 2.2 %collective-permute-done.13.refs_14_ = bf16[192,384]{1,0:T(8,128)(2,1)S(1)} collective-permute-done((bf16[192,384]{1,0:T(8,128)(2,1)S(1)}, bf16[192,384]{1,0:T(8,128)(2,1)S(1)}, u32[]{:S(2)}, u32[]{:S(2)}) %collective-permute-start.13) | collective-permute-done | bytes 147488 | tf_op jit(solution)/shard_map/ppermute | solution.py:38
  35.3 3.3 %collective-permute-start.17 = (bf16[256,1536]{1,0:T(8,128)(2,1)S(1)}, bf16[256,1536]{1,0:T(8,128)(2,1)S(1)}, u32[]{:S(2)}, u32[]{:S(2)}) collective-permute-start(bf16[256,1536]{1,0:T(8,128)(2,1)S(1)} %collective-permute-done.16.refs_0_), channel_id=1, source_target_pairs={{0,2},{2,0},{1,3},{3,1},{4,6},{6,4},{5,7},{7,5},{8,10},{10,8},{9,1... | collective-permute-start | bytes 2359304 | tf_op jit(solution)/shard_map/ppermute | solution.py:38
  38.6 0.0 collective-permute-start.27
  38.6 0.4 collective-permute-start.14
  39.0 1.1 %collective-permute-start.15 = (bf16[192,384]{1,0:T(8,128)(2,1)S(1)}, bf16[192,384]{1,0:T(8,128)(2,1)S(1)}, u32[]{:S(2)}, u32[]{:S(2)}) collective-permute-start(bf16[192,384]{1,0:T(8,128)(2,1)S(1)} %collective-permute-done.12.refs_17_), channel_id=1, source_target_pairs={{0,1},{1,0},{2,3},{3,2},{4,5},{5,4},{6,7},{7,6},{8,9},{9,8},{10,11... | collective-permute-start | bytes 442376 | tf_op jit(solution)/shard_map/ppermute | solution.py:38
  40.1 3.4 %collective-permute-done.14.refs_16_ = bf16[192,384]{1,0:T(8,128)(2,1)S(1)} collective-permute-done((bf16[192,384]{1,0:T(8,128)(2,1)S(1)}, bf16[192,384]{1,0:T(8,128)(2,1)S(1)}, u32[]{:S(2)}, u32[]{:S(2)}) %collective-permute-start.14) | collective-permute-done | bytes 147488 | tf_op jit(solution)/shard_map/ppermute | solution.py:38
  43.5 3.2 %collective-permute-done.15.refs_18_ = bf16[192,384]{1,0:T(8,128)(2,1)S(1)} collective-permute-done((bf16[192,384]{1,0:T(8,128)(2,1)S(1)}, bf16[192,384]{1,0:T(8,128)(2,1)S(1)}, u32[]{:S(2)}, u32[]{:S(2)}) %collective-permute-start.15) | collective-permute-done | bytes 147488 | tf_op jit(solution)/shard_map/ppermute | solution.py:38
  46.7 1.3 %shard_map.65 = (bf16[256,128]{1,0:T(8,128)(2,1)S(1)}, bf16[256,256]{1,0:T(8,128)(2,1)S(1)}, bf16[3072,384]{1,0:T(8,128)(2,1)S(1)}) custom-call(bf16[256,3072]{1,0:T(8,128)(2,1)S(1)} %shard_map.64.refs_0_, f32[1,128]{1,0:T(1,128)S(1)} %bitcast.25, f32[1,128]{1,0:T(1,128)S(1)} %bitcast.27, bf16[192,384]{1,0:T(8,128)(2,1)S(1)} %bitcast.21, ...), custom_call_target="tpu_custom_call" | custom-call | tf_op jit(solution)/shard_map/pallas_call | solution.py:18
  47.9 2.2 %collective-permute-start.19 = (bf16[256,256]{1,0:T(8,128)(2,1)S(1)}, bf16[256,256]{1,0:T(8,128)(2,1)S(1)}, u32[]{:S(2)}, u32[]{:S(2)}) collective-permute-start(bf16[256,256]{1,0:T(8,128)(2,1)S(1)} %get-tuple-element.41.refs_2_), channel_id=1, source_target_pairs={{0,16},{4,20},{8,24},{12,28},{16,0},{20,4},{24,8},{28,12},{1,17},{... | collective-permute-start | bytes 393224 | tf_op jit(solution)/shard_map/ppermute | solution.py:38
  50.1 2.5 %shard_map.66 = (bf16[256,128]{1,0:T(8,128)(2,1)S(1)}, bf16[256,256]{1,0:T(8,128)(2,1)S(1)}) custom-call(bf16[256,1536]{1,0:T(8,128)(2,1)S(1)} %collective-permute-done.16.refs_0_, bf16[256,1536]{1,0:T(8,128)(2,1)S(1)} %collective-permute-done.17.refs_1_, bf16[3,3072]{1,0:T(4,128)(2,1)S(1)} %bitcast.23, f32[1,128]{1,0:T(1,128)S(1)} %bitcast.26, ...), custom_call_target="tpu_custom_call" | custom-call | tf_op jit(solution)/shard_map/pallas_call | solution.py:18
  52.6 0.3 collective-permute-start.22
  52.9 1.2 %collective-permute-start.18 = (bf16[256,256]{1,0:T(8,128)(2,1)S(1)}, bf16[256,256]{1,0:T(8,128)(2,1)S(1)}, u32[]{:S(2)}, u32[]{:S(2)}) collective-permute-start(bf16[256,256]{1,0:T(8,128)(2,1)S(1)} %get-tuple-element.41.refs_2_), channel_id=1, source_target_pairs={{0,8},{4,12},{8,0},{12,4},{16,24},{20,28},{24,16},{28,20},{1,9},{5... | collective-permute-start | bytes 393224 | tf_op jit(solution)/shard_map/ppermute | solution.py:38
  54.1 3.5 %collective-permute-done.19.refs_4_ = bf16[256,256]{1,0:T(8,128)(2,1)S(1)} collective-permute-done((bf16[256,256]{1,0:T(8,128)(2,1)S(1)}, bf16[256,256]{1,0:T(8,128)(2,1)S(1)}, u32[]{:S(2)}, u32[]{:S(2)}) %collective-permute-start.19) | collective-permute-done | bytes 131104 | tf_op jit(solution)/shard_map/ppermute | solution.py:38
  57.6 0.0 collective-permute-start.20
  57.6 1.5 %collective-permute-start.21 = (bf16[256,256]{1,0:T(8,128)(2,1)S(1)}, bf16[256,256]{1,0:T(8,128)(2,1)S(1)}, u32[]{:S(2)}, u32[]{:S(2)}) collective-permute-start(bf16[256,256]{1,0:T(8,128)(2,1)S(1)} %get-tuple-element.42.refs_6_), channel_id=1, source_target_pairs={{0,8},{4,12},{8,0},{12,4},{16,24},{20,28},{24,16},{28,20},{1,9},{5... | collective-permute-start | bytes 393224 | tf_op jit(solution)/shard_map/ppermute | solution.py:38
  59.1 2.8 %collective-permute-done.22.refs_8_ = bf16[256,256]{1,0:T(8,128)(2,1)S(1)} collective-permute-done((bf16[256,256]{1,0:T(8,128)(2,1)S(1)}, bf16[256,256]{1,0:T(8,128)(2,1)S(1)}, u32[]{:S(2)}, u32[]{:S(2)}) %collective-permute-start.22) | collective-permute-done | bytes 131104 | tf_op jit(solution)/shard_map/ppermute | solution.py:38
  61.9 0.0 collective-permute-start.23
  61.9 0.0 collective-permute-done.18.refs_3_
  61.9 2.1 %collective-permute-done.20.refs_5_ = bf16[256,256]{1,0:T(8,128)(2,1)S(1)} collective-permute-done((bf16[256,256]{1,0:T(8,128)(2,1)S(1)}, bf16[256,256]{1,0:T(8,128)(2,1)S(1)}, u32[]{:S(2)}, u32[]{:S(2)}) %collective-permute-start.20) | collective-permute-done | bytes 131104 | tf_op jit(solution)/shard_map/ppermute | solution.py:38
  64.0 2.5 %collective-permute-done.21.refs_7_ = bf16[256,256]{1,0:T(8,128)(2,1)S(1)} collective-permute-done((bf16[256,256]{1,0:T(8,128)(2,1)S(1)}, bf16[256,256]{1,0:T(8,128)(2,1)S(1)}, u32[]{:S(2)}, u32[]{:S(2)}) %collective-permute-start.21) | collective-permute-done | bytes 131104 | tf_op jit(solution)/shard_map/ppermute | solution.py:38
  66.5 2.8 %collective-permute-done.23.refs_9_ = bf16[256,256]{1,0:T(8,128)(2,1)S(1)} collective-permute-done((bf16[256,256]{1,0:T(8,128)(2,1)S(1)}, bf16[256,256]{1,0:T(8,128)(2,1)S(1)}, u32[]{:S(2)}, u32[]{:S(2)}) %collective-permute-start.23) | collective-permute-done | bytes 131104 | tf_op jit(solution)/shard_map/ppermute | solution.py:38
  69.3 2.2 %shard_map.67 = (bf16[256,128]{1,0:T(8,128)(2,1)S(1)}, bf16[256,128]{1,0:T(8,128)(2,1)S(1)}) custom-call(bf16[256,128]{1,0:T(8,128)(2,1)S(1)} %get-tuple-element.36.refs_0_, bf16[256,128]{1,0:T(8,128)(2,1)S(1)} %get-tuple-element.40.refs_1_, bf16[256,256]{1,0:T(8,128)(2,1)S(1)} %get-tuple-element.41.refs_2_, ...), custom_call_target="tpu_custom_call" | custom-call | tf_op jit(solution)/shard_map/pallas_call | solution.py:18
  71.5 1.3 %collective-permute-start.24 = (bf16[256,128]{1,0:T(8,128)(2,1)S(1)}, bf16[256,128]{1,0:T(8,128)(2,1)S(1)}, u32[]{:S(2)}, u32[]{:S(2)}) collective-permute-start(bf16[256,128]{1,0:T(8,128)(2,1)S(1)} %get-tuple-element.44), channel_id=1, source_target_pairs={{0,4},{2,6},{4,0},{6,2},{8,12},{10,14},{12,8},{14,10},{16,20},{18,... | collective-permute-start | bytes 196616 | tf_op jit(solution)/shard_map/ppermute | solution.py:38
  72.8 2.6 %collective-permute-start.25 = (bf16[256,128]{1,0:T(8,128)(2,1)S(1)}, bf16[256,128]{1,0:T(8,128)(2,1)S(1)}, u32[]{:S(2)}, u32[]{:S(2)}) collective-permute-start(bf16[256,128]{1,0:T(8,128)(2,1)S(1)} %get-tuple-element.43.refs_0_), channel_id=1, source_target_pairs={{0,2},{2,0},{4,6},{6,4},{8,10},{10,8},{12,14},{14,12},{16,18},{18,... | collective-permute-start | bytes 196616 | tf_op jit(solution)/shard_map/ppermute | solution.py:38
  75.4 0.2 collective-permute-start.26
  75.6 0.7 collective-permute-done.25.refs_2_
  76.3 2.8 %collective-permute-done.26.refs_3_ = bf16[256,128]{1,0:T(8,128)(2,1)S(1)} collective-permute-done((bf16[256,128]{1,0:T(8,128)(2,1)S(1)}, bf16[256,128]{1,0:T(8,128)(2,1)S(1)}, u32[]{:S(2)}, u32[]{:S(2)}) %collective-permute-start.26) | collective-permute-done | bytes 65568 | tf_op jit(solution)/shard_map/ppermute | solution.py:38
  79.1 1.5 %shard_map.68 = bf16[256,1536]{1,0:T(8,128)(2,1)} custom-call(bf16[256,128]{1,0:T(8,128)(2,1)S(1)} %get-tuple-element.43.refs_0_, bf16[256,128]{1,0:T(8,128)(2,1)S(1)} %collective-permute-done.24.refs_1_, bf16[256,128]{1,0:T(8,128)(2,1)S(1)} %collective-permute-done.25.refs_2_, bf16[256,128]{1,0:T(8,128)(2,1)S(1)} %collective-permute-done.26.refs_3_, ...), custom_call_target="tpu_custom_call" | custom-call | tf_op jit(solution)/shard_map/pallas_call | solution.py:18
  (13 shorter events, 0.1 us)
Async XLA Ops:
  0.0 19.4 %copy-start.1 = (bf16[1,256,1536]{2,1,0:T(8,128)(2,1)S(1)}, bf16[1,256,1536]{2,1,0:T(8,128)(2,1)}, u32[]{:S(2)}) copy-start(bf16[1,256,1536]{2,1,0:T(8,128)(2,1)} %param.6) | copy-start | bytes 2359300
  0.0 17.2 %collective-permute-start = (bf16[256,1536]{1,0:T(8,128)(2,1)}, bf16[256,1536]{1,0:T(8,128)(2,1)S(1)}, u32[]{:S(2)}, u32[]{:S(2)}) collective-permute-start(bf16[256,1536]{1,0:T(8,128)(2,1)} %bitcast.15), channel_id=1, source_target_pairs={{0,2},{2,0},{1,3},{3,1},{4,6},{6,4},{5,7},{7,5},{8,10},{10,8},{9,1... | collective-permute-start | bytes 2359304 | tf_op jit(solution)/shard_map/ppermute | solution.py:38
  1.2 7.6 %collective-permute-start.1 = (bf16[192,384]{1,0:T(8,128)(2,1)S(1)}, bf16[192,384]{1,0:T(8,128)(2,1)S(1)}, u32[]{:S(2)}, u32[]{:S(2)}) collective-permute-start(bf16[192,384]{1,0:T(8,128)(2,1)S(1)} %bitcast.18), channel_id=1, source_target_pairs={{0,1},{1,0},{2,3},{3,2},{4,5},{5,4},{6,7},{7,6},{8,9},{9,8},{10,11... | collective-permute-start | bytes 442376 | tf_op jit(solution)/shard_map/ppermute | solution.py:38
  3.9 5.2 %collective-permute-start.2 = (bf16[192,384]{1,0:T(8,128)(2,1)S(1)}, bf16[192,384]{1,0:T(8,128)(2,1)S(1)}, u32[]{:S(2)}, u32[]{:S(2)}) collective-permute-start(bf16[192,384]{1,0:T(8,128)(2,1)S(1)} %bitcast.29), channel_id=1, source_target_pairs={{0,4},{4,0},{8,12},{12,8},{16,20},{20,16},{24,28},{28,24},{1,5},{5... | collective-permute-start | bytes 442376 | tf_op jit(solution)/shard_map/ppermute | solution.py:38
  5.2 4.8 %collective-permute-start.4 = (bf16[192,384]{1,0:T(8,128)(2,1)S(1)}, bf16[192,384]{1,0:T(8,128)(2,1)S(1)}, u32[]{:S(2)}, u32[]{:S(2)}) collective-permute-start(bf16[192,384]{1,0:T(8,128)(2,1)S(1)} %bitcast.19), channel_id=1, source_target_pairs={{0,8},{4,12},{8,0},{12,4},{16,24},{20,28},{24,16},{28,20},{1,9},{5... | collective-permute-start | bytes 442376 | tf_op jit(solution)/shard_map/ppermute | solution.py:38
  6.5 6.0 %collective-permute-start.5 = (bf16[192,384]{1,0:T(8,128)(2,1)S(1)}, bf16[192,384]{1,0:T(8,128)(2,1)S(1)}, u32[]{:S(2)}, u32[]{:S(2)}) collective-permute-start(bf16[192,384]{1,0:T(8,128)(2,1)S(1)} %bitcast.20), channel_id=1, source_target_pairs={{0,16},{4,20},{8,24},{12,28},{16,0},{20,4},{24,8},{28,12},{1,17},{... | collective-permute-start | bytes 442376 | tf_op jit(solution)/shard_map/ppermute | solution.py:38
  12.5 20.5 %collective-permute-start.16 = (bf16[256,1536]{1,0:T(8,128)(2,1)}, bf16[256,1536]{1,0:T(8,128)(2,1)S(1)}, u32[]{:S(2)}, u32[]{:S(2)}) collective-permute-start(bf16[256,1536]{1,0:T(8,128)(2,1)} %bitcast.16), channel_id=1, source_target_pairs={{0,4},{4,0},{8,12},{12,8},{16,20},{20,16},{24,28},{28,24},{1,5},{5... | collective-permute-start | bytes 2359304 | tf_op jit(solution)/shard_map/ppermute | solution.py:38
  12.8 11.6 %collective-permute-start.6 = (bf16[192,384]{1,0:T(8,128)(2,1)S(1)}, bf16[192,384]{1,0:T(8,128)(2,1)S(1)}, u32[]{:S(2)}, u32[]{:S(2)}) collective-permute-start(bf16[192,384]{1,0:T(8,128)(2,1)S(1)} %collective-permute-done.4.refs_7_), channel_id=1, source_target_pairs={{0,1},{1,0},{2,3},{3,2},{4,5},{5,4},{6,7},{7,6},{8,9},{9,8},{10,11... | collective-permute-start | bytes 442376 | tf_op jit(solution)/shard_map/ppermute | solution.py:38
  13.0 8.7 %collective-permute-start.3 = (bf16[192,384]{1,0:T(8,128)(2,1)S(1)}, bf16[192,384]{1,0:T(8,128)(2,1)S(1)}, u32[]{:S(2)}, u32[]{:S(2)}) collective-permute-start(bf16[192,384]{1,0:T(8,128)(2,1)S(1)} %collective-permute-done.2.refs_5_), channel_id=1, source_target_pairs={{0,1},{1,0},{2,3},{3,2},{4,5},{5,4},{6,7},{7,6},{8,9},{9,8},{10,11... | collective-permute-start | bytes 442376 | tf_op jit(solution)/shard_map/ppermute | solution.py:38
  14.2 8.2 %collective-permute-start.7 = (bf16[192,384]{1,0:T(8,128)(2,1)S(1)}, bf16[192,384]{1,0:T(8,128)(2,1)S(1)}, u32[]{:S(2)}, u32[]{:S(2)}) collective-permute-start(bf16[192,384]{1,0:T(8,128)(2,1)S(1)} %collective-permute-done.2.refs_5_), channel_id=1, source_target_pairs={{0,8},{4,12},{8,0},{12,4},{16,24},{20,28},{24,16},{28,20},{1,9},{5... | collective-permute-start | bytes 442376 | tf_op jit(solution)/shard_map/ppermute | solution.py:38
  17.2 6.3 %collective-permute-start.8 = (bf16[192,384]{1,0:T(8,128)(2,1)S(1)}, bf16[192,384]{1,0:T(8,128)(2,1)S(1)}, u32[]{:S(2)}, u32[]{:S(2)}) collective-permute-start(bf16[192,384]{1,0:T(8,128)(2,1)S(1)} %collective-permute-done.2.refs_5_), channel_id=1, source_target_pairs={{0,16},{4,20},{8,24},{12,28},{16,0},{20,4},{24,8},{28,12},{1,17},{... | collective-permute-start | bytes 442376 | tf_op jit(solution)/shard_map/ppermute | solution.py:38
  19.4 0.7 copy-start.2
  20.2 1.4 %copy-start = (bf16[256,3072]{1,0:T(8,128)(2,1)S(1)}, bf16[256,3072]{1,0:T(8,128)(2,1)}, u32[]{:S(2)}) copy-start(bf16[256,3072]{1,0:T(8,128)(2,1)} %refs_4_.1) | copy-start | bytes 4718596
  21.6 25.1 %copy-start.4 = (f32[128]{0:T(128)S(1)}, f32[128]{0:T(128)}, u32[]{:S(2)}) copy-start(f32[128]{0:T(128)} %param.9) | copy-start | bytes 1540
  21.6 25.0 %copy-start.5 = (f32[128]{0:T(128)S(1)}, f32[128]{0:T(128)}, u32[]{:S(2)}) copy-start(f32[128]{0:T(128)} %param.10) | copy-start | bytes 1540
  21.7 5.9 %collective-permute-start.10 = (bf16[192,384]{1,0:T(8,128)(2,1)S(1)}, bf16[192,384]{1,0:T(8,128)(2,1)S(1)}, u32[]{:S(2)}, u32[]{:S(2)}) collective-permute-start(bf16[192,384]{1,0:T(8,128)(2,1)S(1)} %collective-permute-done.5.refs_11_), channel_id=1, source_target_pairs={{0,8},{4,12},{8,0},{12,4},{16,24},{20,28},{24,16},{28,20},{1,9},{5... | collective-permute-start | bytes 442376 | tf_op jit(solution)/shard_map/ppermute | solution.py:38
  23.5 4.3 %collective-permute-start.9 = (bf16[192,384]{1,0:T(8,128)(2,1)S(1)}, bf16[192,384]{1,0:T(8,128)(2,1)S(1)}, u32[]{:S(2)}, u32[]{:S(2)}) collective-permute-start(bf16[192,384]{1,0:T(8,128)(2,1)S(1)} %collective-permute-done.7.refs_9_), channel_id=1, source_target_pairs={{0,1},{1,0},{2,3},{3,2},{4,5},{5,4},{6,7},{7,6},{8,9},{9,8},{10,11... | collective-permute-start | bytes 442376 | tf_op jit(solution)/shard_map/ppermute | solution.py:38
  23.7 6.7 %collective-permute-start.12 = (bf16[192,384]{1,0:T(8,128)(2,1)S(1)}, bf16[192,384]{1,0:T(8,128)(2,1)S(1)}, u32[]{:S(2)}, u32[]{:S(2)}) collective-permute-start(bf16[192,384]{1,0:T(8,128)(2,1)S(1)} %collective-permute-done.8.refs_13_), channel_id=1, source_target_pairs={{0,8},{4,12},{8,0},{12,4},{16,24},{20,28},{24,16},{28,20},{1,9},{5... | collective-permute-start | bytes 442376 | tf_op jit(solution)/shard_map/ppermute | solution.py:38
  27.6 5.4 %collective-permute-start.11 = (bf16[192,384]{1,0:T(8,128)(2,1)S(1)}, bf16[192,384]{1,0:T(8,128)(2,1)S(1)}, u32[]{:S(2)}, u32[]{:S(2)}) collective-permute-start(bf16[192,384]{1,0:T(8,128)(2,1)S(1)} %collective-permute-done.5.refs_11_), channel_id=1, source_target_pairs={{0,1},{1,0},{2,3},{3,2},{4,5},{5,4},{6,7},{7,6},{8,9},{9,8},{10,11... | collective-permute-start | bytes 442376 | tf_op jit(solution)/shard_map/ppermute | solution.py:38
  30.4 4.9 %collective-permute-start.13 = (bf16[192,384]{1,0:T(8,128)(2,1)S(1)}, bf16[192,384]{1,0:T(8,128)(2,1)S(1)}, u32[]{:S(2)}, u32[]{:S(2)}) collective-permute-start(bf16[192,384]{1,0:T(8,128)(2,1)S(1)} %collective-permute-done.8.refs_13_), channel_id=1, source_target_pairs={{0,1},{1,0},{2,3},{3,2},{4,5},{5,4},{6,7},{7,6},{8,9},{9,8},{10,11... | collective-permute-start | bytes 442376 | tf_op jit(solution)/shard_map/ppermute | solution.py:38
  35.3 14.8 %collective-permute-start.17 = (bf16[256,1536]{1,0:T(8,128)(2,1)S(1)}, bf16[256,1536]{1,0:T(8,128)(2,1)S(1)}, u32[]{:S(2)}, u32[]{:S(2)}) collective-permute-start(bf16[256,1536]{1,0:T(8,128)(2,1)S(1)} %collective-permute-done.16.refs_0_), channel_id=1, source_target_pairs={{0,2},{2,0},{1,3},{3,1},{4,6},{6,4},{5,7},{7,5},{8,10},{10,8},{9,1... | collective-permute-start | bytes 2359304 | tf_op jit(solution)/shard_map/ppermute | solution.py:38
  38.6 37.0 %collective-permute-start.27 = (bf16[256,1536]{1,0:T(8,128)(2,1)S(1)}, bf16[256,1536]{1,0:T(8,128)(2,1)S(1)}, u32[]{:S(2)}, u32[]{:S(2)}) collective-permute-start(bf16[256,1536]{1,0:T(8,128)(2,1)S(1)} %constant_dynamic-slice_fusion), channel_id=1, source_target_pairs={{0,2},{2,0},{1,3},{3,1},{4,6},{6,4},{5,7},{7,5},{8,10},{10,8},{9,1... | collective-permute-start | bytes 2359304 | tf_op jit(solution)/shard_map/ppermute | solution.py:38
  38.6 4.9 %collective-permute-start.14 = (bf16[192,384]{1,0:T(8,128)(2,1)S(1)}, bf16[192,384]{1,0:T(8,128)(2,1)S(1)}, u32[]{:S(2)}, u32[]{:S(2)}) collective-permute-start(bf16[192,384]{1,0:T(8,128)(2,1)S(1)} %collective-permute-done.10.refs_15_), channel_id=1, source_target_pairs={{0,1},{1,0},{2,3},{3,2},{4,5},{5,4},{6,7},{7,6},{8,9},{9,8},{10,11... | collective-permute-start | bytes 442376 | tf_op jit(solution)/shard_map/ppermute | solution.py:38
  39.0 7.7 %collective-permute-start.15 = (bf16[192,384]{1,0:T(8,128)(2,1)S(1)}, bf16[192,384]{1,0:T(8,128)(2,1)S(1)}, u32[]{:S(2)}, u32[]{:S(2)}) collective-permute-start(bf16[192,384]{1,0:T(8,128)(2,1)S(1)} %collective-permute-done.12.refs_17_), channel_id=1, source_target_pairs={{0,1},{1,0},{2,3},{3,2},{4,5},{5,4},{6,7},{7,6},{8,9},{9,8},{10,11... | collective-permute-start | bytes 442376 | tf_op jit(solution)/shard_map/ppermute | solution.py:38
  47.9 9.7 %collective-permute-start.19 = (bf16[256,256]{1,0:T(8,128)(2,1)S(1)}, bf16[256,256]{1,0:T(8,128)(2,1)S(1)}, u32[]{:S(2)}, u32[]{:S(2)}) collective-permute-start(bf16[256,256]{1,0:T(8,128)(2,1)S(1)} %get-tuple-element.41.refs_2_), channel_id=1, source_target_pairs={{0,16},{4,20},{8,24},{12,28},{16,0},{20,4},{24,8},{28,12},{1,17},{... | collective-permute-start | bytes 393224 | tf_op jit(solution)/shard_map/ppermute | solution.py:38
  50.1 29.0 %copy-start.3 = (bf16[1,3,3072]{2,1,0:T(4,128)(2,1)S(1)}, bf16[1,3,3072]{2,1,0:T(4,128)(2,1)}, u32[]{:S(2)}) copy-start(bf16[1,3,3072]{2,1,0:T(4,128)(2,1)} %param.7) | copy-start | bytes 55300
  52.6 9.2 %collective-permute-start.22 = (bf16[256,256]{1,0:T(8,128)(2,1)S(1)}, bf16[256,256]{1,0:T(8,128)(2,1)S(1)}, u32[]{:S(2)}, u32[]{:S(2)}) collective-permute-start(bf16[256,256]{1,0:T(8,128)(2,1)S(1)} %get-tuple-element.42.refs_6_), channel_id=1, source_target_pairs={{0,16},{4,20},{8,24},{12,28},{16,0},{20,4},{24,8},{28,12},{1,17},{... | collective-permute-start | bytes 393224 | tf_op jit(solution)/shard_map/ppermute | solution.py:38
  52.9 8.9 %collective-permute-start.18 = (bf16[256,256]{1,0:T(8,128)(2,1)S(1)}, bf16[256,256]{1,0:T(8,128)(2,1)S(1)}, u32[]{:S(2)}, u32[]{:S(2)}) collective-permute-start(bf16[256,256]{1,0:T(8,128)(2,1)S(1)} %get-tuple-element.41.refs_2_), channel_id=1, source_target_pairs={{0,8},{4,12},{8,0},{12,4},{16,24},{20,28},{24,16},{28,20},{1,9},{5... | collective-permute-start | bytes 393224 | tf_op jit(solution)/shard_map/ppermute | solution.py:38
  57.6 6.4 %collective-permute-start.20 = (bf16[256,256]{1,0:T(8,128)(2,1)S(1)}, bf16[256,256]{1,0:T(8,128)(2,1)S(1)}, u32[]{:S(2)}, u32[]{:S(2)}) collective-permute-start(bf16[256,256]{1,0:T(8,128)(2,1)S(1)} %collective-permute-done.19.refs_4_), channel_id=1, source_target_pairs={{0,8},{4,12},{8,0},{12,4},{16,24},{20,28},{24,16},{28,20},{1,9},{5... | collective-permute-start | bytes 393224 | tf_op jit(solution)/shard_map/ppermute | solution.py:38
  57.6 8.9 %collective-permute-start.21 = (bf16[256,256]{1,0:T(8,128)(2,1)S(1)}, bf16[256,256]{1,0:T(8,128)(2,1)S(1)}, u32[]{:S(2)}, u32[]{:S(2)}) collective-permute-start(bf16[256,256]{1,0:T(8,128)(2,1)S(1)} %get-tuple-element.42.refs_6_), channel_id=1, source_target_pairs={{0,8},{4,12},{8,0},{12,4},{16,24},{20,28},{24,16},{28,20},{1,9},{5... | collective-permute-start | bytes 393224 | tf_op jit(solution)/shard_map/ppermute | solution.py:38
  61.9 7.5 %collective-permute-start.23 = (bf16[256,256]{1,0:T(8,128)(2,1)S(1)}, bf16[256,256]{1,0:T(8,128)(2,1)S(1)}, u32[]{:S(2)}, u32[]{:S(2)}) collective-permute-start(bf16[256,256]{1,0:T(8,128)(2,1)S(1)} %collective-permute-done.22.refs_8_), channel_id=1, source_target_pairs={{0,8},{4,12},{8,0},{12,4},{16,24},{20,28},{24,16},{28,20},{1,9},{5... | collective-permute-start | bytes 393224 | tf_op jit(solution)/shard_map/ppermute | solution.py:38
  71.5 4.1 %collective-permute-start.24 = (bf16[256,128]{1,0:T(8,128)(2,1)S(1)}, bf16[256,128]{1,0:T(8,128)(2,1)S(1)}, u32[]{:S(2)}, u32[]{:S(2)}) collective-permute-start(bf16[256,128]{1,0:T(8,128)(2,1)S(1)} %get-tuple-element.44), channel_id=1, source_target_pairs={{0,4},{2,6},{4,0},{6,2},{8,12},{10,14},{12,8},{14,10},{16,20},{18,... | collective-permute-start | bytes 196616 | tf_op jit(solution)/shard_map/ppermute | solution.py:38
  72.8 3.5 %collective-permute-start.25 = (bf16[256,128]{1,0:T(8,128)(2,1)S(1)}, bf16[256,128]{1,0:T(8,128)(2,1)S(1)}, u32[]{:S(2)}, u32[]{:S(2)}) collective-permute-start(bf16[256,128]{1,0:T(8,128)(2,1)S(1)} %get-tuple-element.43.refs_0_), channel_id=1, source_target_pairs={{0,2},{2,0},{4,6},{6,4},{8,10},{10,8},{12,14},{14,12},{16,18},{18,... | collective-permute-start | bytes 196616 | tf_op jit(solution)/shard_map/ppermute | solution.py:38
  75.4 3.7 %collective-permute-start.26 = (bf16[256,128]{1,0:T(8,128)(2,1)S(1)}, bf16[256,128]{1,0:T(8,128)(2,1)S(1)}, u32[]{:S(2)}, u32[]{:S(2)}) collective-permute-start(bf16[256,128]{1,0:T(8,128)(2,1)S(1)} %get-tuple-element.44), channel_id=1, source_target_pairs={{0,6},{2,4},{4,2},{6,0},{8,14},{10,12},{12,10},{14,8},{16,22},{18,... | collective-permute-start | bytes 196616 | tf_op jit(solution)/shard_map/ppermute | solution.py:38

commit v2 on v1

--- a/solution.py
+++ b/solution.py
@@ -46,13 +46,20 @@
     return [piece] + [swap(piece, ["head"], [n_head], [j]) for j in range(1, n_head)]
 
 
+def tree(count):
+    known, found = [0], []
+    bit = count // 2
+    while bit:
+        found += [(far ^ bit, far) for far in known]
+        known += [far ^ bit for far in known]
+        bit //= 2
+    return found
+
+
 def spread(piece, n_ctx):
     held = {0: piece}
-    bit = n_ctx // PAIR // 2
-    while bit:
-        for far, one in list(held.items()):
-            held[far ^ bit] = swap(one, ["ctx"], [n_ctx], [bit * PAIR])
-        bit //= 2
+    for far, source in tree(n_ctx // PAIR):
+        held[far] = swap(held[source], ["ctx"], [n_ctx], [(far ^ source) * PAIR])
     return [held[far] for far in range(n_ctx // PAIR)]
 
 
@@ -98,9 +105,9 @@
     kv_ref[:, HDIM:] = out[:, 2 * HDIM :].astype(jnp.bfloat16)
 
 
-def first_qkv_kernel(places, n_grp, *refs):
-    tokens_ref, qgain_ref, kgain_ref = refs[:3]
-    chunks, (q_ref, kv_ref, weights) = refs[3:-3], refs[-3:]
+def qkv_kernel(places, n_grp, *refs):
+    tokens_refs, gains = refs[:PAIR], refs[PAIR : PAIR + 2]
+    chunks, out_refs, weights = refs[PAIR + 2 : -5], refs[-5:-1], refs[-1]
     t = lax.axis_index("ctx")
     g = lax.axis_index("grp")
     rows = chunks[0].shape[0]
@@ -108,16 +115,8 @@
         owner = t ^ (far * PAIR + near)
         start = pl.multiple_of((owner * n_grp + (g ^ fg)) * rows, 16)
         weights[pl.ds(start, rows), :] = chunk[...]
-    project(tokens_ref, (qgain_ref, kgain_ref), weights, q_ref, kv_ref)
-
-
-def norm_qkv_kernel(n_head, *refs):
-    pieces, (mods_ref, qgain_ref, kgain_ref, weights, q_ref, kv_ref, normed) = (
-        refs[:n_head],
-        refs[n_head:],
-    )
-    norm_rows(pieces, mods_ref, normed)
-    project(normed, (qgain_ref, kgain_ref), weights, q_ref, kv_ref)
+    for i, tokens_ref in enumerate(tokens_refs):
+        project(tokens_ref, gains, weights, out_refs[2 * i], out_refs[2 * i + 1])
 
 
 def attend_kernel(count, *refs):
@@ -193,44 +192,46 @@
     ]
     outs = [swap(block, ["head"], [n_head], [j]) for j, block in enumerate(blocks, 1)]
 
-    chunks, places = [], []
-    held = [spread(mine, n_ctx), spread(other, n_ctx)]
-    sent = []
-    for far in range(far_count):
+    found = tree(far_count)
+    ready = [0] + [far for far, unused in found]
+    plan = [found[0], (0, None)]
+    plan = [(near, *step) for near in range(PAIR) for step in plan]
+    plan += [(near, *step) for step in found[1:2] for near in range(PAIR)]
+    for i in range(2, len(found)):
         for near in range(PAIR):
-            piece = held[near][far]
-            if len(sent) == 3:
-                sent[1] += (own_normed, *blocks)
-            if len(sent) >= 2:
-                piece = after(piece, *sent[-2])
-            if 0 < far < far_count - 1:
-                piece = after(piece, held[near][far + 1])
+            plan += [(near, *found[i]), (near, ready[i - 1], None)]
+    plan += [(near, far, None) for far in ready[-2:] for near in range(PAIR)]
+    held = [{0: mine}, {0: other}]
+    chunks, places, results = [], [], [(other,)]
+    for near, far, source in plan:
+        piece = held[near][far if source is None else source]
+        if len(results) >= 5:
+            piece = after(piece, *sum(results[:-4], ()))
+        if source is None:
             got = [swap(piece, ["grp"], [n_grp], [fg]) for fg in range(1, n_grp)]
-            sent.append(tuple(got))
             for fg, chunk in enumerate([held[near][far]] + got):
                 chunks.append(chunk)
                 places.append((far, near, fg))
-    first = (other, held[0][far_count // 2], held[0][1], *sent[0])
-    neighbour = swap(after(tokens, *first), ["ctx"], [n_ctx], [1])
-    neighbour = after(neighbour, *sent[-4], *sent[-3])
+        else:
+            got = [swap(piece, ["ctx"], [n_ctx], [(far ^ source) * PAIR])]
+            held[near][far] = got[0]
+        results.append(tuple(got))
+        if len(results) == len(plan) // 2 - 1:
+            results[-1] += (own_normed, *blocks)
+    neighbour = swap(after(tokens, *results[0], *results[2]), ["ctx"], [n_ctx], [1])
+    neighbour = after(neighbour, *sum(results[:-1], ()))
+    other_normed = call(functools.partial(norm_kernel, n_head), wide)(
+        *all_features(neighbour, n_head), mods
+    )
 
     piece_shape = jax.ShapeDtypeStruct((count, HDIM), jnp.bfloat16)
     pair_shape = jax.ShapeDtypeStruct((count, 2 * HDIM), jnp.bfloat16)
     gains = (query_gain[None], key_gain[None])
-    own_queries, own_kv, weights = call(
-        functools.partial(first_qkv_kernel, places, n_grp),
-        (
-            piece_shape,
-            pair_shape,
-            jax.ShapeDtypeStruct((rows * len(places), 3 * HDIM), jnp.bfloat16),
-        ),
-    )(own_normed, *gains, *chunks)
-    other_queries, other_kv = call(
-        functools.partial(norm_qkv_kernel, n_head),
-        (piece_shape, pair_shape),
-        [pltpu.VMEM(wide.shape, jnp.bfloat16)],
-    )(*all_features(neighbour, n_head), mods, *gains, weights)
-
+    own_queries, own_kv, other_queries, other_kv = call(
+        functools.partial(qkv_kernel, places, n_grp),
+        (piece_shape, pair_shape) * PAIR,
+        [pltpu.VMEM((rows * len(places), 3 * HDIM), jnp.bfloat16)],
+    )(own_normed, other_normed, *gains, *chunks)
     gathered = spread(own_kv, n_ctx) + spread(other_kv, n_ctx)
     att_own, att_other = call(
         functools.partial(attend_kernel, len(gathered)), (piece_shape, piece_shape)

time: 80.9 us -> 85.5 us (1.057)
  waiting for transfers between devices: 39.2 us -> 47.6 us
  starting transfers between devices: 30.5 us -> 27.1 us
    ppermute x28, waiting for transfers between devices: 39.2 us -> 47.6 us  [swap(): return lax.ppermute(value, tuple(axes), perm)]
    ppermute x28, starting transfers between devices: 30.5 us -> 27.1 us  [swap(): return lax.ppermute(value, tuple(axes), perm)]
  transfers between devices with their start and end apart: 28 -> 28, of which waited for: 17 -> 18; matrix products, arithmetic and copies ran while one was open for 1% -> 1% of each run, Pallas kernels for 9% -> 8%
where the time goes in v2:
time: 85.5 us; the launch traced here: 85.3 us
  waiting for transfers between devices  47.6 us (56%)
  starting transfers between devices  27.1 us (32%)
  Pallas kernels  8.59 us (10%)
  local copies, waits for them, and re-layouts  1.93 us (2%)
    ppermute x28, waiting for transfers between devices, swap(): return lax.ppermute(value, tuple(axes), perm)  47.6 us
    ppermute x28, starting transfers between devices, swap(): return lax.ppermute(value, tuple(axes), perm)  27.1 us
    pallas_call x5, Pallas kernels, call(): pl.pallas_call(kernel, out_shape=out_shape, in_specs=[VMEM_SPEC] * len(ar...  8.59 us
    unnamed x13, local copies, waits for them, and re-layouts  1.83 us
  transfers between devices with their start and end apart: 28, of which 18 were waited for; matrix products, arithmetic and copies ran while one was open for 1% of the time, Pallas kernels for 8%

profile of v2, /device:TPU:1, one launch (start us, length us, event | category | flops | bytes accessed | tf_op | source)
XLA Modules:
  0.0 85.3 jit_solution(14415104445782913955)
XLA Ops:
  0.0 0.1 collective-permute-start
  0.1 1.1 %dynamic-slice_bitcast_fusion = (bf16[3,24,8,128]{3,2,1,0:T(8,128)(2,1)S(1)}, bf16[3,24,8,128]{3,2,1,0:T(8,128)(2,1)S(1)}) fusion(bf16[192,3,256]{2,0,1:T(8,128)(2,1)} %param.8, s32[]{:T(128)S(6)} %select_n.18, s32[]{:T(128)S(6)} %select_n.17), kind=kLoop, calls=%fused_computation.2 | loop fusion | bytes 589832
  1.2 2.7 %collective-permute-start.1 = (bf16[192,384]{1,0:T(8,128)(2,1)S(1)}, bf16[192,384]{1,0:T(8,128)(2,1)S(1)}, u32[]{:S(2)}, u32[]{:S(2)}) collective-permute-start(bf16[192,384]{1,0:T(8,128)(2,1)S(1)} %bitcast.27), channel_id=1, source_target_pairs={{0,4},{4,0},{8,12},{12,8},{16,20},{20,16},{24,28},{28,24},{1,5},{5... | collective-permute-start | bytes 442376 | tf_op jit(solution)/shard_map/ppermute | solution.py:38
  3.9 1.3 %collective-permute-start.2 = (bf16[192,384]{1,0:T(8,128)(2,1)S(1)}, bf16[192,384]{1,0:T(8,128)(2,1)S(1)}, u32[]{:S(2)}, u32[]{:S(2)}) collective-permute-start(bf16[192,384]{1,0:T(8,128)(2,1)S(1)} %bitcast.18), channel_id=1, source_target_pairs={{0,1},{1,0},{2,3},{3,2},{4,5},{5,4},{6,7},{7,6},{8,9},{9,8},{10,11... | collective-permute-start | bytes 442376 | tf_op jit(solution)/shard_map/ppermute | solution.py:38
  5.2 2.8 %collective-permute-done.1.refs_6_ = bf16[192,384]{1,0:T(8,128)(2,1)S(1)} collective-permute-done((bf16[192,384]{1,0:T(8,128)(2,1)S(1)}, bf16[192,384]{1,0:T(8,128)(2,1)S(1)}, u32[]{:S(2)}, u32[]{:S(2)}) %collective-permute-start.1) | collective-permute-done | bytes 147488 | tf_op jit(solution)/shard_map/ppermute | solution.py:38
  8.0 1.0 %collective-permute-done.2.refs_5_ = bf16[192,384]{1,0:T(8,128)(2,1)S(1)} collective-permute-done((bf16[192,384]{1,0:T(8,128)(2,1)S(1)}, bf16[192,384]{1,0:T(8,128)(2,1)S(1)}, u32[]{:S(2)}, u32[]{:S(2)}) %collective-permute-start.2) | collective-permute-done | bytes 147488 | tf_op jit(solution)/shard_map/ppermute | solution.py:38
  9.0 0.4 collective-permute-start.3
  9.4 2.2 %collective-permute-start.4 = (bf16[192,384]{1,0:T(8,128)(2,1)S(1)}, bf16[192,384]{1,0:T(8,128)(2,1)S(1)}, u32[]{:S(2)}, u32[]{:S(2)}) collective-permute-start(bf16[192,384]{1,0:T(8,128)(2,1)S(1)} %bitcast.19), channel_id=1, source_target_pairs={{0,16},{4,20},{8,24},{12,28},{16,0},{20,4},{24,8},{28,12},{1,17},{... | collective-permute-start | bytes 442376 | tf_op jit(solution)/shard_map/ppermute | solution.py:38
  11.6 0.2 collective-permute-start.5
  11.7 1.1 %collective-permute-start.6 = (bf16[192,384]{1,0:T(8,128)(2,1)S(1)}, bf16[192,384]{1,0:T(8,128)(2,1)S(1)}, u32[]{:S(2)}, u32[]{:S(2)}) collective-permute-start(bf16[192,384]{1,0:T(8,128)(2,1)S(1)} %collective-permute-done.1.refs_6_), channel_id=1, source_target_pairs={{0,1},{1,0},{2,3},{3,2},{4,5},{5,4},{6,7},{7,6},{8,9},{9,8},{10,11... | collective-permute-start | bytes 442376 | tf_op jit(solution)/shard_map/ppermute | solution.py:38
  12.9 8.5 %collective-permute-done.4.refs_8_ = bf16[192,384]{1,0:T(8,128)(2,1)S(1)} collective-permute-done((bf16[192,384]{1,0:T(8,128)(2,1)S(1)}, bf16[192,384]{1,0:T(8,128)(2,1)S(1)}, u32[]{:S(2)}, u32[]{:S(2)}) %collective-permute-start.4) | collective-permute-done | bytes 147488 | tf_op jit(solution)/shard_map/ppermute | solution.py:38
  21.4 1.3 %collective-permute-start.7 = (bf16[192,384]{1,0:T(8,128)(2,1)S(1)}, bf16[192,384]{1,0:T(8,128)(2,1)S(1)}, u32[]{:S(2)}, u32[]{:S(2)}) collective-permute-start(bf16[192,384]{1,0:T(8,128)(2,1)S(1)} %bitcast.20), channel_id=1, source_target_pairs={{0,8},{4,12},{8,0},{12,4},{16,24},{20,28},{24,16},{28,20},{1,9},{5... | collective-permute-start | bytes 442376 | tf_op jit(solution)/shard_map/ppermute | solution.py:38
  22.7 1.9 %collective-permute-done.5.refs_10_ = bf16[192,384]{1,0:T(8,128)(2,1)S(1)} collective-permute-done((bf16[192,384]{1,0:T(8,128)(2,1)S(1)}, bf16[192,384]{1,0:T(8,128)(2,1)S(1)}, u32[]{:S(2)}, u32[]{:S(2)}) %collective-permute-start.5) | collective-permute-done | bytes 147488 | tf_op jit(solution)/shard_map/ppermute | solution.py:38
  24.6 1.3 %collective-permute-start.8 = (bf16[192,384]{1,0:T(8,128)(2,1)S(1)}, bf16[192,384]{1,0:T(8,128)(2,1)S(1)}, u32[]{:S(2)}, u32[]{:S(2)}) collective-permute-start(bf16[192,384]{1,0:T(8,128)(2,1)S(1)} %collective-permute-done.1.refs_6_), channel_id=1, source_target_pairs={{0,8},{4,12},{8,0},{12,4},{16,24},{20,28},{24,16},{28,20},{1,9},{5... | collective-permute-start | bytes 442376 | tf_op jit(solution)/shard_map/ppermute | solution.py:38
  25.8 0.0 collective-permute-done.6.refs_7_
  25.8 0.2 collective-permute-start.9
  26.0 0.0 collective-permute-done.refs_1_
  26.0 1.1 %collective-permute-start.10 = (bf16[192,384]{1,0:T(8,128)(2,1)S(1)}, bf16[192,384]{1,0:T(8,128)(2,1)S(1)}, u32[]{:S(2)}, u32[]{:S(2)}) collective-permute-start(bf16[192,384]{1,0:T(8,128)(2,1)S(1)} %collective-permute-done.4.refs_8_), channel_id=1, source_target_pairs={{0,1},{1,0},{2,3},{3,2},{4,5},{5,4},{6,7},{7,6},{8,9},{9,8},{10,11... | collective-permute-start | bytes 442376 | tf_op jit(solution)/shard_map/ppermute | solution.py:38
  27.1 0.7 copy-done.2
  27.9 1.4 %shard_map.64.refs_0_ = bf16[256,3072]{1,0:T(8,128)(2,1)S(1)} custom-call(bf16[256,1536]{1,0:T(8,128)(2,1)S(1)} %bitcast.17, bf16[256,1536]{1,0:T(8,128)(2,1)S(1)} %collective-permute-done.refs_1_, bf16[3,3072]{1,0:T(4,128)(2,1)S(1)} %bitcast.22), custom_call_target="tpu_custom_call" | custom-call | tf_op jit(solution)/shard_map/pallas_call | solution.py:18
  29.3 0.0 copy-start.3
  29.3 0.0 collective-permute-done.7.refs_12_
  29.3 1.5 %collective-permute-start.11 = (bf16[192,384]{1,0:T(8,128)(2,1)S(1)}, bf16[192,384]{1,0:T(8,128)(2,1)S(1)}, u32[]{:S(2)}, u32[]{:S(2)}) collective-permute-start(bf16[192,384]{1,0:T(8,128)(2,1)S(1)} %collective-permute-done.5.refs_10_), channel_id=1, source_target_pairs={{0,8},{4,12},{8,0},{12,4},{16,24},{20,28},{24,16},{28,20},{1,9},{5... | collective-permute-start | bytes 442376 | tf_op jit(solution)/shard_map/ppermute | solution.py:38
  30.8 0.1 constant_dynamic-slice_fusion
  30.8 0.0 copy-start.4
  30.8 0.0 copy-start.5
  30.8 0.0 collective-permute-done.8.refs_14_
  30.9 0.6 collective-permute-start.12
  31.4 2.1 %collective-permute-done.9.refs_16_ = bf16[192,384]{1,0:T(8,128)(2,1)S(1)} collective-permute-done((bf16[192,384]{1,0:T(8,128)(2,1)S(1)}, bf16[192,384]{1,0:T(8,128)(2,1)S(1)}, u32[]{:S(2)}, u32[]{:S(2)}) %collective-permute-start.9) | collective-permute-done | bytes 147488 | tf_op jit(solution)/shard_map/ppermute | solution.py:38
  33.6 1.0 %collective-permute-start.13 = (bf16[192,384]{1,0:T(8,128)(2,1)S(1)}, bf16[192,384]{1,0:T(8,128)(2,1)S(1)}, u32[]{:S(2)}, u32[]{:S(2)}) collective-permute-start(bf16[192,384]{1,0:T(8,128)(2,1)S(1)} %collective-permute-done.7.refs_12_), channel_id=1, source_target_pairs={{0,1},{1,0},{2,3},{3,2},{4,5},{5,4},{6,7},{7,6},{8,9},{9,8},{10,11... | collective-permute-start | bytes 442376 | tf_op jit(solution)/shard_map/ppermute | solution.py:38
  34.6 0.0 collective-permute-done.10.refs_9_
  34.6 0.4 collective-permute-start.14
  35.0 1.7 %collective-permute-done.11.refs_18_ = bf16[192,384]{1,0:T(8,128)(2,1)S(1)} collective-permute-done((bf16[192,384]{1,0:T(8,128)(2,1)S(1)}, bf16[192,384]{1,0:T(8,128)(2,1)S(1)}, u32[]{:S(2)}, u32[]{:S(2)}) %collective-permute-start.11) | collective-permute-done | bytes 147488 | tf_op jit(solution)/shard_map/ppermute | solution.py:38
  36.7 1.0 %collective-permute-start.15 = (bf16[192,384]{1,0:T(8,128)(2,1)S(1)}, bf16[192,384]{1,0:T(8,128)(2,1)S(1)}, u32[]{:S(2)}, u32[]{:S(2)}) collective-permute-start(bf16[192,384]{1,0:T(8,128)(2,1)S(1)} %collective-permute-done.9.refs_16_), channel_id=1, source_target_pairs={{0,1},{1,0},{2,3},{3,2},{4,5},{5,4},{6,7},{7,6},{8,9},{9,8},{10,11... | collective-permute-start | bytes 442376 | tf_op jit(solution)/shard_map/ppermute | solution.py:38
  37.8 0.0 collective-permute-done.3.refs_0_
  37.8 0.0 collective-permute-done.12.refs_11_
  37.8 1.0 %collective-permute-done.13.refs_13_ = bf16[192,384]{1,0:T(8,128)(2,1)S(1)} collective-permute-done((bf16[192,384]{1,0:T(8,128)(2,1)S(1)}, bf16[192,384]{1,0:T(8,128)(2,1)S(1)}, u32[]{:S(2)}, u32[]{:S(2)}) %collective-permute-start.13) | collective-permute-done | bytes 147488 | tf_op jit(solution)/shard_map/ppermute | solution.py:38
  38.7 3.1 %collective-permute-done.14.refs_15_ = bf16[192,384]{1,0:T(8,128)(2,1)S(1)} collective-permute-done((bf16[192,384]{1,0:T(8,128)(2,1)S(1)}, bf16[192,384]{1,0:T(8,128)(2,1)S(1)}, u32[]{:S(2)}, u32[]{:S(2)}) %collective-permute-start.14) | collective-permute-done | bytes 147488 | tf_op jit(solution)/shard_map/ppermute | solution.py:38
  41.8 3.2 %collective-permute-done.15.refs_17_ = bf16[192,384]{1,0:T(8,128)(2,1)S(1)} collective-permute-done((bf16[192,384]{1,0:T(8,128)(2,1)S(1)}, bf16[192,384]{1,0:T(8,128)(2,1)S(1)}, u32[]{:S(2)}, u32[]{:S(2)}) %collective-permute-start.15) | collective-permute-done | bytes 147488 | tf_op jit(solution)/shard_map/ppermute | solution.py:38
  45.0 2.8 %collective-permute-start.16 = (bf16[256,1536]{1,0:T(8,128)(2,1)S(1)}, bf16[256,1536]{1,0:T(8,128)(2,1)S(1)}, u32[]{:S(2)}, u32[]{:S(2)}) collective-permute-start(bf16[256,1536]{1,0:T(8,128)(2,1)S(1)} %collective-permute-done.3.refs_0_), channel_id=1, source_target_pairs={{0,2},{2,0},{1,3},{3,1},{4,6},{6,4},{5,7},{7,5},{8,10},{10,8},{9,1... | collective-permute-start | bytes 2359304 | tf_op jit(solution)/shard_map/ppermute | solution.py:38
  47.7 0.0 collective-permute-start.27
  47.7 1.0 %collective-permute-start.17 = (bf16[192,384]{1,0:T(8,128)(2,1)S(1)}, bf16[192,384]{1,0:T(8,128)(2,1)S(1)}, u32[]{:S(2)}, u32[]{:S(2)}) collective-permute-start(bf16[192,384]{1,0:T(8,128)(2,1)S(1)} %collective-permute-done.11.refs_18_), channel_id=1, source_target_pairs={{0,1},{1,0},{2,3},{3,2},{4,5},{5,4},{6,7},{7,6},{8,9},{9,8},{10,11... | collective-permute-start | bytes 442376 | tf_op jit(solution)/shard_map/ppermute | solution.py:38
  48.8 0.9 %collective-permute-done.16.refs_1_ = bf16[256,1536]{1,0:T(8,128)(2,1)S(1)} collective-permute-done((bf16[256,1536]{1,0:T(8,128)(2,1)S(1)}, bf16[256,1536]{1,0:T(8,128)(2,1)S(1)}, u32[]{:S(2)}, u32[]{:S(2)}) %collective-permute-start.16) | collective-permute-done | bytes 786464 | tf_op jit(solution)/shard_map/ppermute | solution.py:38
  49.7 1.4 %shard_map.65.refs_1_ = bf16[256,3072]{1,0:T(8,128)(2,1)S(1)} custom-call(bf16[256,1536]{1,0:T(8,128)(2,1)S(1)} %collective-permute-done.3.refs_0_, bf16[256,1536]{1,0:T(8,128)(2,1)S(1)} %collective-permute-done.16.refs_1_, bf16[3,3072]{1,0:T(4,128)(2,1)S(1)} %bitcast.23), custom_call_target="tpu_custom_call" | custom-call | tf_op jit(solution)/shard_map/pallas_call | solution.py:18
  51.1 1.6 %collective-permute-done.17.refs_19_ = bf16[192,384]{1,0:T(8,128)(2,1)S(1)} collective-permute-done((bf16[192,384]{1,0:T(8,128)(2,1)S(1)}, bf16[192,384]{1,0:T(8,128)(2,1)S(1)}, u32[]{:S(2)}, u32[]{:S(2)}) %collective-permute-start.17) | collective-permute-done | bytes 147488 | tf_op jit(solution)/shard_map/ppermute | solution.py:38
  52.7 2.1 %shard_map.66 = (bf16[256,128]{1,0:T(8,128)(2,1)S(1)}, bf16[256,256]{1,0:T(8,128)(2,1)S(1)}, bf16[256,128]{1,0:T(8,128)(2,1)S(1)}, bf16[256,256]{1,0:T(8,128)(2,1)S(1)}) custom-call(bf16[256,3072]{1,0:T(8,128)(2,1)S(1)} %shard_map.64.refs_0_, bf16[256,3072]{1,0:T(8,128)(2,1)S(1)} %shard_map.65.refs_1_, f32[1,128]{1,0:T(1,128)S(1)} %bitcast.25, ...), custom_call_target="tpu_custom_call" | custom-call | tf_op jit(solution)/shard_map/pallas_call | solution.py:18
  54.8 2.3 %collective-permute-start.19 = (bf16[256,256]{1,0:T(8,128)(2,1)S(1)}, bf16[256,256]{1,0:T(8,128)(2,1)S(1)}, u32[]{:S(2)}, u32[]{:S(2)}) collective-permute-start(bf16[256,256]{1,0:T(8,128)(2,1)S(1)} %get-tuple-element.39.refs_2_), channel_id=1, source_target_pairs={{0,16},{4,20},{8,24},{12,28},{16,0},{20,4},{24,8},{28,12},{1,17},{... | collective-permute-start | bytes 393224 | tf_op jit(solution)/shard_map/ppermute | solution.py:38
  57.1 0.1 collective-permute-start.22
  57.2 0.8 collective-permute-start.18
  58.0 0.6 collective-permute-start.21
  58.7 7.5 %collective-permute-done.19.refs_4_ = bf16[256,256]{1,0:T(8,128)(2,1)S(1)} collective-permute-done((bf16[256,256]{1,0:T(8,128)(2,1)S(1)}, bf16[256,256]{1,0:T(8,128)(2,1)S(1)}, u32[]{:S(2)}, u32[]{:S(2)}) %collective-permute-start.19) | collective-permute-done | bytes 131104 | tf_op jit(solution)/shard_map/ppermute | solution.py:38
  66.2 2.8 %collective-permute-done.22.refs_8_ = bf16[256,256]{1,0:T(8,128)(2,1)S(1)} collective-permute-done((bf16[256,256]{1,0:T(8,128)(2,1)S(1)}, bf16[256,256]{1,0:T(8,128)(2,1)S(1)}, u32[]{:S(2)}, u32[]{:S(2)}) %collective-permute-start.22) | collective-permute-done | bytes 131104 | tf_op jit(solution)/shard_map/ppermute | solution.py:38
  69.0 0.2 collective-permute-start.23
  69.3 3.3 %collective-permute-done.20.refs_5_ = bf16[256,256]{1,0:T(8,128)(2,1)S(1)} collective-permute-done((bf16[256,256]{1,0:T(8,128)(2,1)S(1)}, bf16[256,256]{1,0:T(8,128)(2,1)S(1)}, u32[]{:S(2)}, u32[]{:S(2)}) %collective-permute-start.20) | collective-permute-done | bytes 131104 | tf_op jit(solution)/shard_map/ppermute | solution.py:38
  72.6 2.8 %collective-permute-done.23.refs_9_ = bf16[256,256]{1,0:T(8,128)(2,1)S(1)} collective-permute-done((bf16[256,256]{1,0:T(8,128)(2,1)S(1)}, bf16[256,256]{1,0:T(8,128)(2,1)S(1)}, u32[]{:S(2)}, u32[]{:S(2)}) %collective-permute-start.23) | collective-permute-done | bytes 131104 | tf_op jit(solution)/shard_map/ppermute | solution.py:38
  75.4 2.2 %shard_map.67 = (bf16[256,128]{1,0:T(8,128)(2,1)S(1)}, bf16[256,128]{1,0:T(8,128)(2,1)S(1)}) custom-call(bf16[256,128]{1,0:T(8,128)(2,1)S(1)} %get-tuple-element.37.refs_0_, bf16[256,128]{1,0:T(8,128)(2,1)S(1)} %get-tuple-element.38.refs_1_, bf16[256,256]{1,0:T(8,128)(2,1)S(1)} %get-tuple-element.39.refs_2_, ...), custom_call_target="tpu_custom_call" | custom-call | tf_op jit(solution)/shard_map/pallas_call | solution.py:18
  77.6 1.0 %collective-permute-start.24 = (bf16[256,128]{1,0:T(8,128)(2,1)S(1)}, bf16[256,128]{1,0:T(8,128)(2,1)S(1)}, u32[]{:S(2)}, u32[]{:S(2)}) collective-permute-start(bf16[256,128]{1,0:T(8,128)(2,1)S(1)} %get-tuple-element.42), channel_id=1, source_target_pairs={{0,4},{2,6},{4,0},{6,2},{8,12},{10,14},{12,8},{14,10},{16,20},{18,... | collective-permute-start | bytes 196616 | tf_op jit(solution)/shard_map/ppermute | solution.py:38
  78.6 1.5 %collective-permute-start.25 = (bf16[256,128]{1,0:T(8,128)(2,1)S(1)}, bf16[256,128]{1,0:T(8,128)(2,1)S(1)}, u32[]{:S(2)}, u32[]{:S(2)}) collective-permute-start(bf16[256,128]{1,0:T(8,128)(2,1)S(1)} %get-tuple-element.41.refs_0_), channel_id=1, source_target_pairs={{0,2},{2,0},{4,6},{6,4},{8,10},{10,8},{12,14},{14,12},{16,18},{18,... | collective-permute-start | bytes 196616 | tf_op jit(solution)/shard_map/ppermute | solution.py:38
  80.1 0.4 collective-permute-start.26
  80.5 0.0 collective-permute-done.27.refs_5_
  80.5 0.3 collective-permute-done.24.refs_1_
  80.8 0.2 collective-permute-done.25.refs_2_
  81.0 2.8 %collective-permute-done.26.refs_3_ = bf16[256,128]{1,0:T(8,128)(2,1)S(1)} collective-permute-done((bf16[256,128]{1,0:T(8,128)(2,1)S(1)}, bf16[256,128]{1,0:T(8,128)(2,1)S(1)}, u32[]{:S(2)}, u32[]{:S(2)}) %collective-permute-start.26) | collective-permute-done | bytes 65568 | tf_op jit(solution)/shard_map/ppermute | solution.py:38
  83.8 1.5 %shard_map.68 = bf16[256,1536]{1,0:T(8,128)(2,1)} custom-call(bf16[256,128]{1,0:T(8,128)(2,1)S(1)} %get-tuple-element.41.refs_0_, bf16[256,128]{1,0:T(8,128)(2,1)S(1)} %collective-permute-done.24.refs_1_, bf16[256,128]{1,0:T(8,128)(2,1)S(1)} %collective-permute-done.25.refs_2_, bf16[256,128]{1,0:T(8,128)(2,1)S(1)} %collective-permute-done.26.refs_3_, ...), custom_call_target="tpu_custom_call" | custom-call | tf_op jit(solution)/shard_map/pallas_call | solution.py:18
  (13 shorter events, 0.1 us)
Async XLA Ops:
  0.0 27.1 %copy-start.1 = (bf16[1,256,1536]{2,1,0:T(8,128)(2,1)S(1)}, bf16[1,256,1536]{2,1,0:T(8,128)(2,1)}, u32[]{:S(2)}) copy-start(bf16[1,256,1536]{2,1,0:T(8,128)(2,1)} %param.6) | copy-start | bytes 2359300
  0.0 26.0 %collective-permute-start = (bf16[256,1536]{1,0:T(8,128)(2,1)}, bf16[256,1536]{1,0:T(8,128)(2,1)S(1)}, u32[]{:S(2)}, u32[]{:S(2)}) collective-permute-start(bf16[256,1536]{1,0:T(8,128)(2,1)} %bitcast.15), channel_id=1, source_target_pairs={{0,2},{2,0},{1,3},{3,1},{4,6},{6,4},{5,7},{7,5},{8,10},{10,8},{9,1... | collective-permute-start | bytes 2359304 | tf_op jit(solution)/shard_map/ppermute | solution.py:38
  1.2 6.8 %collective-permute-start.1 = (bf16[192,384]{1,0:T(8,128)(2,1)S(1)}, bf16[192,384]{1,0:T(8,128)(2,1)S(1)}, u32[]{:S(2)}, u32[]{:S(2)}) collective-permute-start(bf16[192,384]{1,0:T(8,128)(2,1)S(1)} %bitcast.27), channel_id=1, source_target_pairs={{0,4},{4,0},{8,12},{12,8},{16,20},{20,16},{24,28},{28,24},{1,5},{5... | collective-permute-start | bytes 442376 | tf_op jit(solution)/shard_map/ppermute | solution.py:38
  3.9 5.2 %collective-permute-start.2 = (bf16[192,384]{1,0:T(8,128)(2,1)S(1)}, bf16[192,384]{1,0:T(8,128)(2,1)S(1)}, u32[]{:S(2)}, u32[]{:S(2)}) collective-permute-start(bf16[192,384]{1,0:T(8,128)(2,1)S(1)} %bitcast.18), channel_id=1, source_target_pairs={{0,1},{1,0},{2,3},{3,2},{4,5},{5,4},{6,7},{7,6},{8,9},{9,8},{10,11... | collective-permute-start | bytes 442376 | tf_op jit(solution)/shard_map/ppermute | solution.py:38
  9.0 28.7 %collective-permute-start.3 = (bf16[256,1536]{1,0:T(8,128)(2,1)}, bf16[256,1536]{1,0:T(8,128)(2,1)S(1)}, u32[]{:S(2)}, u32[]{:S(2)}) collective-permute-start(bf16[256,1536]{1,0:T(8,128)(2,1)} %bitcast.16), channel_id=1, source_target_pairs={{0,4},{4,0},{8,12},{12,8},{16,20},{20,16},{24,28},{28,24},{1,5},{5... | collective-permute-start | bytes 2359304 | tf_op jit(solution)/shard_map/ppermute | solution.py:38
  9.4 12.0 %collective-permute-start.4 = (bf16[192,384]{1,0:T(8,128)(2,1)S(1)}, bf16[192,384]{1,0:T(8,128)(2,1)S(1)}, u32[]{:S(2)}, u32[]{:S(2)}) collective-permute-start(bf16[192,384]{1,0:T(8,128)(2,1)S(1)} %bitcast.19), channel_id=1, source_target_pairs={{0,16},{4,20},{8,24},{12,28},{16,0},{20,4},{24,8},{28,12},{1,17},{... | collective-permute-start | bytes 442376 | tf_op jit(solution)/shard_map/ppermute | solution.py:38
  11.6 13.0 %collective-permute-start.5 = (bf16[192,384]{1,0:T(8,128)(2,1)S(1)}, bf16[192,384]{1,0:T(8,128)(2,1)S(1)}, u32[]{:S(2)}, u32[]{:S(2)}) collective-permute-start(bf16[192,384]{1,0:T(8,128)(2,1)S(1)} %collective-permute-done.1.refs_6_), channel_id=1, source_target_pairs={{0,16},{4,20},{8,24},{12,28},{16,0},{20,4},{24,8},{28,12},{1,17},{... | collective-permute-start | bytes 442376 | tf_op jit(solution)/shard_map/ppermute | solution.py:38
  11.7 14.1 %collective-permute-start.6 = (bf16[192,384]{1,0:T(8,128)(2,1)S(1)}, bf16[192,384]{1,0:T(8,128)(2,1)S(1)}, u32[]{:S(2)}, u32[]{:S(2)}) collective-permute-start(bf16[192,384]{1,0:T(8,128)(2,1)S(1)} %collective-permute-done.1.refs_6_), channel_id=1, source_target_pairs={{0,1},{1,0},{2,3},{3,2},{4,5},{5,4},{6,7},{7,6},{8,9},{9,8},{10,11... | collective-permute-start | bytes 442376 | tf_op jit(solution)/shard_map/ppermute | solution.py:38
  21.4 7.9 %collective-permute-start.7 = (bf16[192,384]{1,0:T(8,128)(2,1)S(1)}, bf16[192,384]{1,0:T(8,128)(2,1)S(1)}, u32[]{:S(2)}, u32[]{:S(2)}) collective-permute-start(bf16[192,384]{1,0:T(8,128)(2,1)S(1)} %bitcast.20), channel_id=1, source_target_pairs={{0,8},{4,12},{8,0},{12,4},{16,24},{20,28},{24,16},{28,20},{1,9},{5... | collective-permute-start | bytes 442376 | tf_op jit(solution)/shard_map/ppermute | solution.py:38
  24.6 6.3 %collective-permute-start.8 = (bf16[192,384]{1,0:T(8,128)(2,1)S(1)}, bf16[192,384]{1,0:T(8,128)(2,1)S(1)}, u32[]{:S(2)}, u32[]{:S(2)}) collective-permute-start(bf16[192,384]{1,0:T(8,128)(2,1)S(1)} %collective-permute-done.1.refs_6_), channel_id=1, source_target_pairs={{0,8},{4,12},{8,0},{12,4},{16,24},{20,28},{24,16},{28,20},{1,9},{5... | collective-permute-start | bytes 442376 | tf_op jit(solution)/shard_map/ppermute | solution.py:38
  25.8 7.8 %collective-permute-start.9 = (bf16[192,384]{1,0:T(8,128)(2,1)S(1)}, bf16[192,384]{1,0:T(8,128)(2,1)S(1)}, u32[]{:S(2)}, u32[]{:S(2)}) collective-permute-start(bf16[192,384]{1,0:T(8,128)(2,1)S(1)} %collective-permute-done.4.refs_8_), channel_id=1, source_target_pairs={{0,8},{4,12},{8,0},{12,4},{16,24},{20,28},{24,16},{28,20},{1,9},{5... | collective-permute-start | bytes 442376 | tf_op jit(solution)/shard_map/ppermute | solution.py:38
  26.0 8.6 %collective-permute-start.10 = (bf16[192,384]{1,0:T(8,128)(2,1)S(1)}, bf16[192,384]{1,0:T(8,128)(2,1)S(1)}, u32[]{:S(2)}, u32[]{:S(2)}) collective-permute-start(bf16[192,384]{1,0:T(8,128)(2,1)S(1)} %collective-permute-done.4.refs_8_), channel_id=1, source_target_pairs={{0,1},{1,0},{2,3},{3,2},{4,5},{5,4},{6,7},{7,6},{8,9},{9,8},{10,11... | collective-permute-start | bytes 442376 | tf_op jit(solution)/shard_map/ppermute | solution.py:38
  27.1 0.7 copy-start.2
  27.9 2.9 %copy-start = (bf16[256,3072]{1,0:T(8,128)(2,1)S(1)}, bf16[256,3072]{1,0:T(8,128)(2,1)}, u32[]{:S(2)}) copy-start(bf16[256,3072]{1,0:T(8,128)(2,1)} %refs_4_.1) | copy-start | bytes 4718596
  29.3 20.4 %copy-start.3 = (bf16[1,3,3072]{2,1,0:T(4,128)(2,1)S(1)}, bf16[1,3,3072]{2,1,0:T(4,128)(2,1)}, u32[]{:S(2)}) copy-start(bf16[1,3,3072]{2,1,0:T(4,128)(2,1)} %param.7) | copy-start | bytes 55300
  29.3 7.4 %collective-permute-start.11 = (bf16[192,384]{1,0:T(8,128)(2,1)S(1)}, bf16[192,384]{1,0:T(8,128)(2,1)S(1)}, u32[]{:S(2)}, u32[]{:S(2)}) collective-permute-start(bf16[192,384]{1,0:T(8,128)(2,1)S(1)} %collective-permute-done.5.refs_10_), channel_id=1, source_target_pairs={{0,8},{4,12},{8,0},{12,4},{16,24},{20,28},{24,16},{28,20},{1,9},{5... | collective-permute-start | bytes 442376 | tf_op jit(solution)/shard_map/ppermute | solution.py:38
  30.8 21.8 %copy-start.4 = (f32[128]{0:T(128)S(1)}, f32[128]{0:T(128)}, u32[]{:S(2)}) copy-start(f32[128]{0:T(128)} %param.9) | copy-start | bytes 1540
  30.8 21.8 %copy-start.5 = (f32[128]{0:T(128)S(1)}, f32[128]{0:T(128)}, u32[]{:S(2)}) copy-start(f32[128]{0:T(128)} %param.10) | copy-start | bytes 1540
  30.9 6.9 %collective-permute-start.12 = (bf16[192,384]{1,0:T(8,128)(2,1)S(1)}, bf16[192,384]{1,0:T(8,128)(2,1)S(1)}, u32[]{:S(2)}, u32[]{:S(2)}) collective-permute-start(bf16[192,384]{1,0:T(8,128)(2,1)S(1)} %collective-permute-done.5.refs_10_), channel_id=1, source_target_pairs={{0,1},{1,0},{2,3},{3,2},{4,5},{5,4},{6,7},{7,6},{8,9},{9,8},{10,11... | collective-permute-start | bytes 442376 | tf_op jit(solution)/shard_map/ppermute | solution.py:38
  33.6 5.2 %collective-permute-start.13 = (bf16[192,384]{1,0:T(8,128)(2,1)S(1)}, bf16[192,384]{1,0:T(8,128)(2,1)S(1)}, u32[]{:S(2)}, u32[]{:S(2)}) collective-permute-start(bf16[192,384]{1,0:T(8,128)(2,1)S(1)} %collective-permute-done.7.refs_12_), channel_id=1, source_target_pairs={{0,1},{1,0},{2,3},{3,2},{4,5},{5,4},{6,7},{7,6},{8,9},{9,8},{10,11... | collective-permute-start | bytes 442376 | tf_op jit(solution)/shard_map/ppermute | solution.py:38
  34.6 7.2 %collective-permute-start.14 = (bf16[192,384]{1,0:T(8,128)(2,1)S(1)}, bf16[192,384]{1,0:T(8,128)(2,1)S(1)}, u32[]{:S(2)}, u32[]{:S(2)}) collective-permute-start(bf16[192,384]{1,0:T(8,128)(2,1)S(1)} %collective-permute-done.8.refs_14_), channel_id=1, source_target_pairs={{0,1},{1,0},{2,3},{3,2},{4,5},{5,4},{6,7},{7,6},{8,9},{9,8},{10,11... | collective-permute-start | bytes 442376 | tf_op jit(solution)/shard_map/ppermute | solution.py:38
  36.7 8.2 %collective-permute-start.15 = (bf16[192,384]{1,0:T(8,128)(2,1)S(1)}, bf16[192,384]{1,0:T(8,128)(2,1)S(1)}, u32[]{:S(2)}, u32[]{:S(2)}) collective-permute-start(bf16[192,384]{1,0:T(8,128)(2,1)S(1)} %collective-permute-done.9.refs_16_), channel_id=1, source_target_pairs={{0,1},{1,0},{2,3},{3,2},{4,5},{5,4},{6,7},{7,6},{8,9},{9,8},{10,11... | collective-permute-start | bytes 442376 | tf_op jit(solution)/shard_map/ppermute | solution.py:38
  45.0 4.7 %collective-permute-start.16 = (bf16[256,1536]{1,0:T(8,128)(2,1)S(1)}, bf16[256,1536]{1,0:T(8,128)(2,1)S(1)}, u32[]{:S(2)}, u32[]{:S(2)}) collective-permute-start(bf16[256,1536]{1,0:T(8,128)(2,1)S(1)} %collective-permute-done.3.refs_0_), channel_id=1, source_target_pairs={{0,2},{2,0},{1,3},{3,1},{4,6},{6,4},{5,7},{7,5},{8,10},{10,8},{9,1... | collective-permute-start | bytes 2359304 | tf_op jit(solution)/shard_map/ppermute | solution.py:38
  47.7 32.7 %collective-permute-start.27 = (bf16[256,1536]{1,0:T(8,128)(2,1)S(1)}, bf16[256,1536]{1,0:T(8,128)(2,1)S(1)}, u32[]{:S(2)}, u32[]{:S(2)}) collective-permute-start(bf16[256,1536]{1,0:T(8,128)(2,1)S(1)} %constant_dynamic-slice_fusion), channel_id=1, source_target_pairs={{0,2},{2,0},{1,3},{3,1},{4,6},{6,4},{5,7},{7,5},{8,10},{10,8},{9,1... | collective-permute-start | bytes 2359304 | tf_op jit(solution)/shard_map/ppermute | solution.py:38
  47.7 4.9 %collective-permute-start.17 = (bf16[192,384]{1,0:T(8,128)(2,1)S(1)}, bf16[192,384]{1,0:T(8,128)(2,1)S(1)}, u32[]{:S(2)}, u32[]{:S(2)}) collective-permute-start(bf16[192,384]{1,0:T(8,128)(2,1)S(1)} %collective-permute-done.11.refs_18_), channel_id=1, source_target_pairs={{0,1},{1,0},{2,3},{3,2},{4,5},{5,4},{6,7},{7,6},{8,9},{9,8},{10,11... | collective-permute-start | bytes 442376 | tf_op jit(solution)/shard_map/ppermute | solution.py:38
  54.8 11.4 %collective-permute-start.19 = (bf16[256,256]{1,0:T(8,128)(2,1)S(1)}, bf16[256,256]{1,0:T(8,128)(2,1)S(1)}, u32[]{:S(2)}, u32[]{:S(2)}) collective-permute-start(bf16[256,256]{1,0:T(8,128)(2,1)S(1)} %get-tuple-element.39.refs_2_), channel_id=1, source_target_pairs={{0,16},{4,20},{8,24},{12,28},{16,0},{20,4},{24,8},{28,12},{1,17},{... | collective-permute-start | bytes 393224 | tf_op jit(solution)/shard_map/ppermute | solution.py:38
  57.1 12.0 %collective-permute-start.22 = (bf16[256,256]{1,0:T(8,128)(2,1)S(1)}, bf16[256,256]{1,0:T(8,128)(2,1)S(1)}, u32[]{:S(2)}, u32[]{:S(2)}) collective-permute-start(bf16[256,256]{1,0:T(8,128)(2,1)S(1)} %get-tuple-element.40.refs_6_), channel_id=1, source_target_pairs={{0,16},{4,20},{8,24},{12,28},{16,0},{20,4},{24,8},{28,12},{1,17},{... | collective-permute-start | bytes 393224 | tf_op jit(solution)/shard_map/ppermute | solution.py:38
  57.2 12.1 %collective-permute-start.18 = (bf16[256,256]{1,0:T(8,128)(2,1)S(1)}, bf16[256,256]{1,0:T(8,128)(2,1)S(1)}, u32[]{:S(2)}, u32[]{:S(2)}) collective-permute-start(bf16[256,256]{1,0:T(8,128)(2,1)S(1)} %get-tuple-element.39.refs_2_), channel_id=1, source_target_pairs={{0,8},{4,12},{8,0},{12,4},{16,24},{20,28},{24,16},{28,20},{1,9},{5... | collective-permute-start | bytes 393224 | tf_op jit(solution)/shard_map/ppermute | solution.py:38
  58.0 11.3 %collective-permute-start.21 = (bf16[256,256]{1,0:T(8,128)(2,1)S(1)}, bf16[256,256]{1,0:T(8,128)(2,1)S(1)}, u32[]{:S(2)}, u32[]{:S(2)}) collective-permute-start(bf16[256,256]{1,0:T(8,128)(2,1)S(1)} %get-tuple-element.40.refs_6_), channel_id=1, source_target_pairs={{0,8},{4,12},{8,0},{12,4},{16,24},{20,28},{24,16},{28,20},{1,9},{5... | collective-permute-start | bytes 393224 | tf_op jit(solution)/shard_map/ppermute | solution.py:38
  66.2 6.4 %collective-permute-start.20 = (bf16[256,256]{1,0:T(8,128)(2,1)S(1)}, bf16[256,256]{1,0:T(8,128)(2,1)S(1)}, u32[]{:S(2)}, u32[]{:S(2)}) collective-permute-start(bf16[256,256]{1,0:T(8,128)(2,1)S(1)} %collective-permute-done.19.refs_4_), channel_id=1, source_target_pairs={{0,8},{4,12},{8,0},{12,4},{16,24},{20,28},{24,16},{28,20},{1,9},{5... | collective-permute-start | bytes 393224 | tf_op jit(solution)/shard_map/ppermute | solution.py:38
  69.0 6.4 %collective-permute-start.23 = (bf16[256,256]{1,0:T(8,128)(2,1)S(1)}, bf16[256,256]{1,0:T(8,128)(2,1)S(1)}, u32[]{:S(2)}, u32[]{:S(2)}) collective-permute-start(bf16[256,256]{1,0:T(8,128)(2,1)S(1)} %collective-permute-done.22.refs_8_), channel_id=1, source_target_pairs={{0,8},{4,12},{8,0},{12,4},{16,24},{20,28},{24,16},{28,20},{1,9},{5... | collective-permute-start | bytes 393224 | tf_op jit(solution)/shard_map/ppermute | solution.py:38
  77.6 3.2 %collective-permute-start.24 = (bf16[256,128]{1,0:T(8,128)(2,1)S(1)}, bf16[256,128]{1,0:T(8,128)(2,1)S(1)}, u32[]{:S(2)}, u32[]{:S(2)}) collective-permute-start(bf16[256,128]{1,0:T(8,128)(2,1)S(1)} %get-tuple-element.42), channel_id=1, source_target_pairs={{0,4},{2,6},{4,0},{6,2},{8,12},{10,14},{12,8},{14,10},{16,20},{18,... | collective-permute-start | bytes 196616 | tf_op jit(solution)/shard_map/ppermute | solution.py:38
  78.6 2.4 %collective-permute-start.25 = (bf16[256,128]{1,0:T(8,128)(2,1)S(1)}, bf16[256,128]{1,0:T(8,128)(2,1)S(1)}, u32[]{:S(2)}, u32[]{:S(2)}) collective-permute-start(bf16[256,128]{1,0:T(8,128)(2,1)S(1)} %get-tuple-element.41.refs_0_), channel_id=1, source_target_pairs={{0,2},{2,0},{4,6},{6,4},{8,10},{10,8},{12,14},{14,12},{16,18},{18,... | collective-permute-start | bytes 196616 | tf_op jit(solution)/shard_map/ppermute | solution.py:38
  80.1 3.7 %collective-permute-start.26 = (bf16[256,128]{1,0:T(8,128)(2,1)S(1)}, bf16[256,128]{1,0:T(8,128)(2,1)S(1)}, u32[]{:S(2)}, u32[]{:S(2)}) collective-permute-start(bf16[256,128]{1,0:T(8,128)(2,1)S(1)} %get-tuple-element.42), channel_id=1, source_target_pairs={{0,6},{2,4},{4,2},{6,0},{8,14},{10,12},{12,10},{14,8},{16,22},{18,... | collective-permute-start | bytes 196616 | tf_op jit(solution)/shard_map/ppermute | solution.py:38

commit v3 on v2

--- a/solution.py
+++ b/solution.py
@@ -110,11 +110,12 @@
     chunks, out_refs, weights = refs[PAIR + 2 : -5], refs[-5:-1], refs[-1]
     t = lax.axis_index("ctx")
     g = lax.axis_index("grp")
-    rows = chunks[0].shape[0]
-    for (far, near, fg), chunk in zip(places, chunks):
-        owner = t ^ (far * PAIR + near)
-        start = pl.multiple_of((owner * n_grp + (g ^ fg)) * rows, 16)
-        weights[pl.ds(start, rows), :] = chunk[...]
+    rows = chunks[0].shape[0] // PAIR
+    for (far, fg), chunk in zip(places, chunks):
+        for near in range(PAIR):
+            owner = t ^ (far * PAIR + near)
+            start = pl.multiple_of((owner * n_grp + (g ^ fg)) * rows, 16)
+            weights[pl.ds(start, rows), :] = chunk[near * rows : (near + 1) * rows, :]
     for i, tokens_ref in enumerate(tokens_refs):
         project(tokens_ref, gains, weights, out_refs[2 * i], out_refs[2 * i + 1])
 
@@ -193,33 +194,25 @@
     outs = [swap(block, ["head"], [n_head], [j]) for j, block in enumerate(blocks, 1)]
 
     found = tree(far_count)
-    ready = [0] + [far for far, unused in found]
-    plan = [found[0], (0, None)]
-    plan = [(near, *step) for near in range(PAIR) for step in plan]
-    plan += [(near, *step) for step in found[1:2] for near in range(PAIR)]
-    for i in range(2, len(found)):
-        for near in range(PAIR):
-            plan += [(near, *found[i]), (near, ready[i - 1], None)]
-    plan += [(near, far, None) for far in ready[-2:] for near in range(PAIR)]
-    held = [{0: mine}, {0: other}]
-    chunks, places, results = [], [], [(other,)]
-    for near, far, source in plan:
-        piece = held[near][far if source is None else source]
-        if len(results) >= 5:
-            piece = after(piece, *sum(results[:-4], ()))
-        if source is None:
-            got = [swap(piece, ["grp"], [n_grp], [fg]) for fg in range(1, n_grp)]
-            for fg, chunk in enumerate([held[near][far]] + got):
-                chunks.append(chunk)
-                places.append((far, near, fg))
-        else:
-            got = [swap(piece, ["ctx"], [n_ctx], [(far ^ source) * PAIR])]
-            held[near][far] = got[0]
-        results.append(tuple(got))
-        if len(results) == len(plan) // 2 - 1:
-            results[-1] += (own_normed, *blocks)
-    neighbour = swap(after(tokens, *results[0], *results[2]), ["ctx"], [n_ctx], [1])
-    neighbour = after(neighbour, *sum(results[:-1], ()))
+    top = found[0][0]
+    halves = [swap(piece, ["ctx"], [n_ctx], [top * PAIR]) for piece in (mine, other)]
+    held = {0: jnp.concatenate([mine, other]), top: jnp.concatenate(halves)}
+    for far, source in found[1:]:
+        held[far] = swap(held[source], ["ctx"], [n_ctx], [(far ^ source) * PAIR])
+    chunks, places, sent = [], [], []
+    order = sorted(range(far_count), key=lambda far: (far.bit_count(), far))
+    for i, far in enumerate(order):
+        waits = sent[i - 2] if i >= 2 else ()
+        if i == 2:
+            waits += (own_normed, *blocks, held[order[1]])
+        piece = after(held[far], *waits)
+        got = [swap(piece, ["grp"], [n_grp], [fg]) for fg in range(1, n_grp)]
+        sent.append(tuple(got))
+        for fg, chunk in enumerate([held[far]] + got):
+            chunks.append(chunk)
+            places.append((far, fg))
+    neighbour = swap(after(tokens, other, halves[0]), ["ctx"], [n_ctx], [1])
+    neighbour = after(neighbour, *sent[-3], *sent[-2], held[order[-1]])
     other_normed = call(functools.partial(norm_kernel, n_head), wide)(
         *all_features(neighbour, n_head), mods
     )
@@ -230,7 +223,7 @@
     own_queries, own_kv, other_queries, other_kv = call(
         functools.partial(qkv_kernel, places, n_grp),
         (piece_shape, pair_shape) * PAIR,
-        [pltpu.VMEM((rows * len(places), 3 * HDIM), jnp.bfloat16)],
+        [pltpu.VMEM((PAIR * rows * len(places), 3 * HDIM), jnp.bfloat16)],
     )(own_normed, other_normed, *gains, *chunks)
     gathered = spread(own_kv, n_ctx) + spread(other_kv, n_ctx)
     att_own, att_other = call(

time: 85.5 us -> 78.3 us (0.916)
  waiting for transfers between devices: 47.6 us -> 35.5 us
  starting transfers between devices: 27.1 us -> 31.9 us
    ppermute x28 -> x22, waiting for transfers between devices: 47.6 us -> 35.5 us  [swap(): return lax.ppermute(value, tuple(axes), perm)]
    ppermute x28 -> x22, starting transfers between devices: 27.1 us -> 31.9 us  [swap(): return lax.ppermute(value, tuple(axes), perm)]
  transfers between devices with their start and end apart: 28 -> 22, of which waited for: 18 -> 15; matrix products, arithmetic and copies ran while one was open for 1% -> 2% of each run, Pallas kernels for 8% -> 9%
where the time goes in v3:
time: 78.3 us; the launch traced here: 77.4 us
  waiting for transfers between devices  35.5 us (45%)
  starting transfers between devices  31.9 us (41%)
  Pallas kernels  8.6 us (11%)
  local copies, waits for them, and re-layouts  1.28 us (2%)
    ppermute x22, waiting for transfers between devices, swap(): return lax.ppermute(value, tuple(axes), perm)  35.5 us
    ppermute x22, starting transfers between devices, swap(): return lax.ppermute(value, tuple(axes), perm)  31.9 us
    pallas_call x5, Pallas kernels, call(): pl.pallas_call(kernel, out_shape=out_shape, in_specs=[VMEM_SPEC] * len(ar...  8.6 us
  transfers between devices with their start and end apart: 22, of which 15 were waited for; matrix products, arithmetic and copies ran while one was open for 2% of the time, Pallas kernels for 9%

profile of v3, /device:TPU:1, one launch (start us, length us, event | category | flops | bytes accessed | tf_op | source)
XLA Modules:
  0.0 77.4 jit_solution(2629728426913239608)
XLA Ops:
  0.0 0.0 copy-start.1
  0.0 0.0 copy-start.2
  0.0 0.1 collective-permute-start
  0.1 1.1 %dynamic-slice_bitcast_fusion = (bf16[3,24,8,128]{3,2,1,0:T(8,128)(2,1)S(1)}, bf16[3,24,8,128]{3,2,1,0:T(8,128)(2,1)S(1)}) fusion(bf16[192,3,256]{2,0,1:T(8,128)(2,1)} %param.8, s32[]{:T(128)S(6)} %select_n.18, s32[]{:T(128)S(6)} %select_n.17), kind=kLoop, calls=%fused_computation.2 | loop fusion | bytes 589832
  1.2 3.8 %collective-permute-start.2 = (bf16[192,384]{1,0:T(8,128)(2,1)S(1)}, bf16[192,384]{1,0:T(8,128)(2,1)S(1)}, u32[]{:S(2)}, u32[]{:S(2)}) collective-permute-start(bf16[192,384]{1,0:T(8,128)(2,1)S(1)} %bitcast.25), channel_id=1, source_target_pairs={{0,16},{4,20},{8,24},{12,28},{16,0},{20,4},{24,8},{28,12},{1,17},{... | collective-permute-start | bytes 442376 | tf_op jit(solution)/shard_map/ppermute | solution.py:38
  5.0 1.3 %collective-permute-start.1 = (bf16[192,384]{1,0:T(8,128)(2,1)S(1)}, bf16[192,384]{1,0:T(8,128)(2,1)S(1)}, u32[]{:S(2)}, u32[]{:S(2)}) collective-permute-start(bf16[192,384]{1,0:T(8,128)(2,1)S(1)} %bitcast.26), channel_id=1, source_target_pairs={{0,4},{4,0},{8,12},{12,8},{16,20},{20,16},{24,28},{28,24},{1,5},{5... | collective-permute-start | bytes 442376 | tf_op jit(solution)/shard_map/ppermute | solution.py:38
  6.3 3.8 %collective-permute-done.1 = bf16[192,384]{1,0:T(8,128)(2,1)S(1)} collective-permute-done((bf16[192,384]{1,0:T(8,128)(2,1)S(1)}, bf16[192,384]{1,0:T(8,128)(2,1)S(1)}, u32[]{:S(2)}, u32[]{:S(2)}) %collective-permute-start.1) | collective-permute-done | bytes 147488 | tf_op jit(solution)/shard_map/ppermute | solution.py:38
  10.1 1.4 %collective-permute-start.4 = (bf16[384,384]{1,0:T(8,128)(2,1)S(1)}, bf16[384,384]{1,0:T(8,128)(2,1)S(1)}, u32[]{:S(2)}, u32[]{:S(2)}) collective-permute-start(bf16[384,384]{1,0:T(8,128)(2,1)S(1)} %constant_dynamic-update-slice_fusion.refs_4_), channel_id=1, source_target_pairs={{0,8},{4,12},{8,0},{12,4},{16,24},{20,28},{24,16},{28,20},{1,9},{5... | collective-permute-start | bytes 884744 | tf_op jit(solution)/shard_map/ppermute | solution.py:38
  11.5 0.1 collective-permute-start.6
  11.6 0.6 collective-permute-done.2
  12.2 0.0 copy-done.1
  12.2 1.1 %collective-permute-start.3 = (bf16[256,1536]{1,0:T(8,128)(2,1)S(1)}, bf16[256,1536]{1,0:T(8,128)(2,1)S(1)}, u32[]{:S(2)}, u32[]{:S(2)}) collective-permute-start(bf16[256,1536]{1,0:T(8,128)(2,1)S(1)} %bitcast.18), channel_id=1, source_target_pairs={{0,4},{4,0},{8,12},{12,8},{16,20},{20,16},{24,28},{28,24},{1,5},{5... | collective-permute-start | bytes 2359304 | tf_op jit(solution)/shard_map/ppermute | solution.py:38
  13.3 1.2 %collective-permute-start.7 = (bf16[384,384]{1,0:T(8,128)(2,1)S(1)}, bf16[384,384]{1,0:T(8,128)(2,1)S(1)}, u32[]{:S(2)}, u32[]{:S(2)}) collective-permute-start(bf16[384,384]{1,0:T(8,128)(2,1)S(1)} %constant_dynamic-update-slice_fusion.refs_4_), channel_id=1, source_target_pairs={{0,1},{1,0},{2,3},{3,2},{4,5},{5,4},{6,7},{7,6},{8,9},{9,8},{10,11... | collective-permute-start | bytes 884744 | tf_op jit(solution)/shard_map/ppermute | solution.py:38
  14.6 5.2 %collective-permute-done.6 = bf16[192,384]{1,0:T(8,128)(2,1)S(1)} collective-permute-done((bf16[192,384]{1,0:T(8,128)(2,1)S(1)}, bf16[192,384]{1,0:T(8,128)(2,1)S(1)}, u32[]{:S(2)}, u32[]{:S(2)}) %collective-permute-start.6) | collective-permute-done | bytes 147488 | tf_op jit(solution)/shard_map/ppermute | solution.py:38
  19.8 1.6 %collective-permute-start.9 = (bf16[384,384]{1,0:T(8,128)(2,1)S(1)}, bf16[384,384]{1,0:T(8,128)(2,1)S(1)}, u32[]{:S(2)}, u32[]{:S(2)}) collective-permute-start(bf16[384,384]{1,0:T(8,128)(2,1)S(1)} %constant_dynamic-update-slice_fusion.2.refs_8_), channel_id=1, source_target_pairs={{0,8},{4,12},{8,0},{12,4},{16,24},{20,28},{24,16},{28,20},{1,9},{5... | collective-permute-start | bytes 884744 | tf_op jit(solution)/shard_map/ppermute | solution.py:38
  21.4 0.0 collective-permute-done.4.refs_6_
  21.5 0.5 collective-permute-start.5
  21.9 0.0 collective-permute-done.refs_1_
  21.9 0.0 copy-done.2
  21.9 0.0 copy-start
  21.9 1.4 %shard_map.64.refs_0_ = bf16[256,3072]{1,0:T(8,128)(2,1)S(1)} custom-call(bf16[256,1536]{1,0:T(8,128)(2,1)S(1)} %bitcast.19, bf16[256,1536]{1,0:T(8,128)(2,1)S(1)} %collective-permute-done.refs_1_, bf16[3,3072]{1,0:T(4,128)(2,1)S(1)} %bitcast.20), custom_call_target="tpu_custom_call" | custom-call | tf_op jit(solution)/shard_map/pallas_call | solution.py:18
  23.3 0.0 copy-done
  23.3 0.1 constant_dynamic-slice_fusion
  23.4 0.0 copy-start.3
  23.4 0.0 copy-start.4
  23.4 0.0 collective-permute-done.7.refs_5_
  23.4 1.1 %collective-permute-start.8 = (bf16[384,384]{1,0:T(8,128)(2,1)S(1)}, bf16[384,384]{1,0:T(8,128)(2,1)S(1)}, u32[]{:S(2)}, u32[]{:S(2)}) collective-permute-start(bf16[384,384]{1,0:T(8,128)(2,1)S(1)} %constant_dynamic-update-slice_fusion.2.refs_8_), channel_id=1, source_target_pairs={{0,1},{1,0},{2,3},{3,2},{4,5},{5,4},{6,7},{7,6},{8,9},{9,8},{10,11... | collective-permute-start | bytes 884744 | tf_op jit(solution)/shard_map/ppermute | solution.py:38
  24.5 2.0 %collective-permute-done.9.refs_10_ = bf16[384,384]{1,0:T(8,128)(2,1)S(1)} collective-permute-done((bf16[384,384]{1,0:T(8,128)(2,1)S(1)}, bf16[384,384]{1,0:T(8,128)(2,1)S(1)}, u32[]{:S(2)}, u32[]{:S(2)}) %collective-permute-start.9) | collective-permute-done | bytes 294944 | tf_op jit(solution)/shard_map/ppermute | solution.py:38
  26.5 1.4 %collective-permute-done.5.refs_7_ = bf16[384,384]{1,0:T(8,128)(2,1)S(1)} collective-permute-done((bf16[384,384]{1,0:T(8,128)(2,1)S(1)}, bf16[384,384]{1,0:T(8,128)(2,1)S(1)}, u32[]{:S(2)}, u32[]{:S(2)}) %collective-permute-start.5) | collective-permute-done | bytes 294944 | tf_op jit(solution)/shard_map/ppermute | solution.py:38
  27.9 2.2 %collective-permute-done.3.refs_0_ = bf16[256,1536]{1,0:T(8,128)(2,1)S(1)} collective-permute-done((bf16[256,1536]{1,0:T(8,128)(2,1)S(1)}, bf16[256,1536]{1,0:T(8,128)(2,1)S(1)}, u32[]{:S(2)}, u32[]{:S(2)}) %collective-permute-start.3) | collective-permute-done | bytes 786464 | tf_op jit(solution)/shard_map/ppermute | solution.py:38
  30.1 4.1 %collective-permute-done.8.refs_9_ = bf16[384,384]{1,0:T(8,128)(2,1)S(1)} collective-permute-done((bf16[384,384]{1,0:T(8,128)(2,1)S(1)}, bf16[384,384]{1,0:T(8,128)(2,1)S(1)}, u32[]{:S(2)}, u32[]{:S(2)}) %collective-permute-start.8) | collective-permute-done | bytes 294944 | tf_op jit(solution)/shard_map/ppermute | solution.py:38
  34.2 3.0 %collective-permute-start.10 = (bf16[256,1536]{1,0:T(8,128)(2,1)S(1)}, bf16[256,1536]{1,0:T(8,128)(2,1)S(1)}, u32[]{:S(2)}, u32[]{:S(2)}) collective-permute-start(bf16[256,1536]{1,0:T(8,128)(2,1)S(1)} %collective-permute-done.3.refs_0_), channel_id=1, source_target_pairs={{0,2},{2,0},{1,3},{3,1},{4,6},{6,4},{5,7},{7,5},{8,10},{10,8},{9,1... | collective-permute-start | bytes 2359304 | tf_op jit(solution)/shard_map/ppermute | solution.py:38
  37.2 0.0 collective-permute-start.21
  37.2 0.5 collective-permute-start.11
  37.7 1.4 %collective-permute-done.10.refs_1_ = bf16[256,1536]{1,0:T(8,128)(2,1)S(1)} collective-permute-done((bf16[256,1536]{1,0:T(8,128)(2,1)S(1)}, bf16[256,1536]{1,0:T(8,128)(2,1)S(1)}, u32[]{:S(2)}, u32[]{:S(2)}) %collective-permute-start.10) | collective-permute-done | bytes 786464 | tf_op jit(solution)/shard_map/ppermute | solution.py:38
  39.1 1.4 %shard_map.65.refs_1_ = bf16[256,3072]{1,0:T(8,128)(2,1)S(1)} custom-call(bf16[256,1536]{1,0:T(8,128)(2,1)S(1)} %collective-permute-done.3.refs_0_, bf16[256,1536]{1,0:T(8,128)(2,1)S(1)} %collective-permute-done.10.refs_1_, bf16[3,3072]{1,0:T(4,128)(2,1)S(1)} %bitcast.21), custom_call_target="tpu_custom_call" | custom-call | tf_op jit(solution)/shard_map/pallas_call | solution.py:18
  40.5 4.8 %collective-permute-done.11.refs_11_ = bf16[384,384]{1,0:T(8,128)(2,1)S(1)} collective-permute-done((bf16[384,384]{1,0:T(8,128)(2,1)S(1)}, bf16[384,384]{1,0:T(8,128)(2,1)S(1)}, u32[]{:S(2)}, u32[]{:S(2)}) %collective-permute-start.11) | collective-permute-done | bytes 294944 | tf_op jit(solution)/shard_map/ppermute | solution.py:38
  45.3 0.0 copy-done.3
  45.3 0.0 copy-done.4
  45.3 2.1 %shard_map.66 = (bf16[256,128]{1,0:T(8,128)(2,1)S(1)}, bf16[256,256]{1,0:T(8,128)(2,1)S(1)}, bf16[256,128]{1,0:T(8,128)(2,1)S(1)}, bf16[256,256]{1,0:T(8,128)(2,1)S(1)}) custom-call(bf16[256,3072]{1,0:T(8,128)(2,1)S(1)} %shard_map.64.refs_0_, bf16[256,3072]{1,0:T(8,128)(2,1)S(1)} %shard_map.65.refs_1_, f32[1,128]{1,0:T(1,128)S(1)} %bitcast.23, ...), custom_call_target="tpu_custom_call" | custom-call | tf_op jit(solution)/shard_map/pallas_call | solution.py:18
  47.4 1.8 %collective-permute-start.13 = (bf16[256,256]{1,0:T(8,128)(2,1)S(1)}, bf16[256,256]{1,0:T(8,128)(2,1)S(1)}, u32[]{:S(2)}, u32[]{:S(2)}) collective-permute-start(bf16[256,256]{1,0:T(8,128)(2,1)S(1)} %get-tuple-element.23.refs_2_), channel_id=1, source_target_pairs={{0,16},{4,20},{8,24},{12,28},{16,0},{20,4},{24,8},{28,12},{1,17},{... | collective-permute-start | bytes 393224 | tf_op jit(solution)/shard_map/ppermute | solution.py:38
  49.2 0.6 collective-permute-start.16
  49.8 1.7 %collective-permute-start.12 = (bf16[256,256]{1,0:T(8,128)(2,1)S(1)}, bf16[256,256]{1,0:T(8,128)(2,1)S(1)}, u32[]{:S(2)}, u32[]{:S(2)}) collective-permute-start(bf16[256,256]{1,0:T(8,128)(2,1)S(1)} %get-tuple-element.23.refs_2_), channel_id=1, source_target_pairs={{0,8},{4,12},{8,0},{12,4},{16,24},{20,28},{24,16},{28,20},{1,9},{5... | collective-permute-start | bytes 393224 | tf_op jit(solution)/shard_map/ppermute | solution.py:38
  51.5 0.0 collective-permute-start.15
  51.6 0.6 collective-permute-done.13.refs_4_
  52.2 6.9 %collective-permute-start.14 = (bf16[256,256]{1,0:T(8,128)(2,1)S(1)}, bf16[256,256]{1,0:T(8,128)(2,1)S(1)}, u32[]{:S(2)}, u32[]{:S(2)}) collective-permute-start(bf16[256,256]{1,0:T(8,128)(2,1)S(1)} %collective-permute-done.13.refs_4_), channel_id=1, source_target_pairs={{0,8},{4,12},{8,0},{12,4},{16,24},{20,28},{24,16},{28,20},{1,9},{5... | collective-permute-start | bytes 393224 | tf_op jit(solution)/shard_map/ppermute | solution.py:38
  59.1 1.8 %collective-permute-done.16.refs_8_ = bf16[256,256]{1,0:T(8,128)(2,1)S(1)} collective-permute-done((bf16[256,256]{1,0:T(8,128)(2,1)S(1)}, bf16[256,256]{1,0:T(8,128)(2,1)S(1)}, u32[]{:S(2)}, u32[]{:S(2)}) %collective-permute-start.16) | collective-permute-done | bytes 131104 | tf_op jit(solution)/shard_map/ppermute | solution.py:38
  60.9 1.2 %collective-permute-start.17 = (bf16[256,256]{1,0:T(8,128)(2,1)S(1)}, bf16[256,256]{1,0:T(8,128)(2,1)S(1)}, u32[]{:S(2)}, u32[]{:S(2)}) collective-permute-start(bf16[256,256]{1,0:T(8,128)(2,1)S(1)} %collective-permute-done.16.refs_8_), channel_id=1, source_target_pairs={{0,8},{4,12},{8,0},{12,4},{16,24},{20,28},{24,16},{28,20},{1,9},{5... | collective-permute-start | bytes 393224 | tf_op jit(solution)/shard_map/ppermute | solution.py:38
  62.1 0.0 collective-permute-done.12.refs_3_
  62.1 0.0 collective-permute-done.15.refs_7_
  62.1 1.6 %collective-permute-done.14.refs_5_ = bf16[256,256]{1,0:T(8,128)(2,1)S(1)} collective-permute-done((bf16[256,256]{1,0:T(8,128)(2,1)S(1)}, bf16[256,256]{1,0:T(8,128)(2,1)S(1)}, u32[]{:S(2)}, u32[]{:S(2)}) %collective-permute-start.14) | collective-permute-done | bytes 131104 | tf_op jit(solution)/shard_map/ppermute | solution.py:38
  63.7 2.5 %collective-permute-done.17.refs_9_ = bf16[256,256]{1,0:T(8,128)(2,1)S(1)} collective-permute-done((bf16[256,256]{1,0:T(8,128)(2,1)S(1)}, bf16[256,256]{1,0:T(8,128)(2,1)S(1)}, u32[]{:S(2)}, u32[]{:S(2)}) %collective-permute-start.17) | collective-permute-done | bytes 131104 | tf_op jit(solution)/shard_map/ppermute | solution.py:38
  66.2 2.2 %shard_map.67 = (bf16[256,128]{1,0:T(8,128)(2,1)S(1)}, bf16[256,128]{1,0:T(8,128)(2,1)S(1)}) custom-call(bf16[256,128]{1,0:T(8,128)(2,1)S(1)} %get-tuple-element.21.refs_0_, bf16[256,128]{1,0:T(8,128)(2,1)S(1)} %get-tuple-element.22.refs_1_, bf16[256,256]{1,0:T(8,128)(2,1)S(1)} %get-tuple-element.23.refs_2_, ...), custom_call_target="tpu_custom_call" | custom-call | tf_op jit(solution)/shard_map/pallas_call | solution.py:18
  68.4 1.2 %collective-permute-start.18 = (bf16[256,128]{1,0:T(8,128)(2,1)S(1)}, bf16[256,128]{1,0:T(8,128)(2,1)S(1)}, u32[]{:S(2)}, u32[]{:S(2)}) collective-permute-start(bf16[256,128]{1,0:T(8,128)(2,1)S(1)} %get-tuple-element.26), channel_id=1, source_target_pairs={{0,4},{2,6},{4,0},{6,2},{8,12},{10,14},{12,8},{14,10},{16,20},{18,... | collective-permute-start | bytes 196616 | tf_op jit(solution)/shard_map/ppermute | solution.py:38
  69.7 2.3 %collective-permute-start.19 = (bf16[256,128]{1,0:T(8,128)(2,1)S(1)}, bf16[256,128]{1,0:T(8,128)(2,1)S(1)}, u32[]{:S(2)}, u32[]{:S(2)}) collective-permute-start(bf16[256,128]{1,0:T(8,128)(2,1)S(1)} %get-tuple-element.25.refs_0_), channel_id=1, source_target_pairs={{0,2},{2,0},{4,6},{6,4},{8,10},{10,8},{12,14},{14,12},{16,18},{18,... | collective-permute-start | bytes 196616 | tf_op jit(solution)/shard_map/ppermute | solution.py:38
  72.0 0.5 collective-permute-start.20
  72.5 0.0 collective-permute-done.21.refs_5_
  72.5 0.0 collective-permute-done.18.refs_1_
  72.5 0.4 collective-permute-done.19.refs_2_
  72.9 3.0 %collective-permute-done.20.refs_3_ = bf16[256,128]{1,0:T(8,128)(2,1)S(1)} collective-permute-done((bf16[256,128]{1,0:T(8,128)(2,1)S(1)}, bf16[256,128]{1,0:T(8,128)(2,1)S(1)}, u32[]{:S(2)}, u32[]{:S(2)}) %collective-permute-start.20) | collective-permute-done | bytes 65568 | tf_op jit(solution)/shard_map/ppermute | solution.py:38
  75.8 1.5 %shard_map.68 = bf16[256,1536]{1,0:T(8,128)(2,1)} custom-call(bf16[256,128]{1,0:T(8,128)(2,1)S(1)} %get-tuple-element.25.refs_0_, bf16[256,128]{1,0:T(8,128)(2,1)S(1)} %collective-permute-done.18.refs_1_, bf16[256,128]{1,0:T(8,128)(2,1)S(1)} %collective-permute-done.19.refs_2_, bf16[256,128]{1,0:T(8,128)(2,1)S(1)} %collective-permute-done.20.refs_3_, ...), custom_call_target="tpu_custom_call" | custom-call | tf_op jit(solution)/shard_map/pallas_call | solution.py:18
  (6 shorter events, 0.1 us)
Async XLA Ops:
  0.0 12.2 %copy-start.1 = (bf16[1,256,1536]{2,1,0:T(8,128)(2,1)S(1)}, bf16[1,256,1536]{2,1,0:T(8,128)(2,1)}, u32[]{:S(2)}) copy-start(bf16[1,256,1536]{2,1,0:T(8,128)(2,1)} %param.6) | copy-start | bytes 2359300
  0.0 21.9 %copy-start.2 = (bf16[1,3,3072]{2,1,0:T(4,128)(2,1)S(1)}, bf16[1,3,3072]{2,1,0:T(4,128)(2,1)}, u32[]{:S(2)}) copy-start(bf16[1,3,3072]{2,1,0:T(4,128)(2,1)} %param.7) | copy-start | bytes 55300
  0.0 21.9 %collective-permute-start = (bf16[256,1536]{1,0:T(8,128)(2,1)}, bf16[256,1536]{1,0:T(8,128)(2,1)S(1)}, u32[]{:S(2)}, u32[]{:S(2)}) collective-permute-start(bf16[256,1536]{1,0:T(8,128)(2,1)} %bitcast.17), channel_id=1, source_target_pairs={{0,2},{2,0},{1,3},{3,1},{4,6},{6,4},{5,7},{7,5},{8,10},{10,8},{9,1... | collective-permute-start | bytes 2359304 | tf_op jit(solution)/shard_map/ppermute | solution.py:38
  1.2 11.0 %collective-permute-start.2 = (bf16[192,384]{1,0:T(8,128)(2,1)S(1)}, bf16[192,384]{1,0:T(8,128)(2,1)S(1)}, u32[]{:S(2)}, u32[]{:S(2)}) collective-permute-start(bf16[192,384]{1,0:T(8,128)(2,1)S(1)} %bitcast.25), channel_id=1, source_target_pairs={{0,16},{4,20},{8,24},{12,28},{16,0},{20,4},{24,8},{28,12},{1,17},{... | collective-permute-start | bytes 442376 | tf_op jit(solution)/shard_map/ppermute | solution.py:38
  5.0 5.1 %collective-permute-start.1 = (bf16[192,384]{1,0:T(8,128)(2,1)S(1)}, bf16[192,384]{1,0:T(8,128)(2,1)S(1)}, u32[]{:S(2)}, u32[]{:S(2)}) collective-permute-start(bf16[192,384]{1,0:T(8,128)(2,1)S(1)} %bitcast.26), channel_id=1, source_target_pairs={{0,4},{4,0},{8,12},{12,8},{16,20},{20,16},{24,28},{28,24},{1,5},{5... | collective-permute-start | bytes 442376 | tf_op jit(solution)/shard_map/ppermute | solution.py:38
  10.1 11.3 %collective-permute-start.4 = (bf16[384,384]{1,0:T(8,128)(2,1)S(1)}, bf16[384,384]{1,0:T(8,128)(2,1)S(1)}, u32[]{:S(2)}, u32[]{:S(2)}) collective-permute-start(bf16[384,384]{1,0:T(8,128)(2,1)S(1)} %constant_dynamic-update-slice_fusion.refs_4_), channel_id=1, source_target_pairs={{0,8},{4,12},{8,0},{12,4},{16,24},{20,28},{24,16},{28,20},{1,9},{5... | collective-permute-start | bytes 884744 | tf_op jit(solution)/shard_map/ppermute | solution.py:38
  11.5 8.3 %collective-permute-start.6 = (bf16[192,384]{1,0:T(8,128)(2,1)S(1)}, bf16[192,384]{1,0:T(8,128)(2,1)S(1)}, u32[]{:S(2)}, u32[]{:S(2)}) collective-permute-start(bf16[192,384]{1,0:T(8,128)(2,1)S(1)} %collective-permute-done.1), channel_id=1, source_target_pairs={{0,16},{4,20},{8,24},{12,28},{16,0},{20,4},{24,8},{28,12},{1,17},{... | collective-permute-start | bytes 442376 | tf_op jit(solution)/shard_map/ppermute | solution.py:38
  12.2 17.9 %collective-permute-start.3 = (bf16[256,1536]{1,0:T(8,128)(2,1)S(1)}, bf16[256,1536]{1,0:T(8,128)(2,1)S(1)}, u32[]{:S(2)}, u32[]{:S(2)}) collective-permute-start(bf16[256,1536]{1,0:T(8,128)(2,1)S(1)} %bitcast.18), channel_id=1, source_target_pairs={{0,4},{4,0},{8,12},{12,8},{16,20},{20,16},{24,28},{28,24},{1,5},{5... | collective-permute-start | bytes 2359304 | tf_op jit(solution)/shard_map/ppermute | solution.py:38
  13.3 10.1 %collective-permute-start.7 = (bf16[384,384]{1,0:T(8,128)(2,1)S(1)}, bf16[384,384]{1,0:T(8,128)(2,1)S(1)}, u32[]{:S(2)}, u32[]{:S(2)}) collective-permute-start(bf16[384,384]{1,0:T(8,128)(2,1)S(1)} %constant_dynamic-update-slice_fusion.refs_4_), channel_id=1, source_target_pairs={{0,1},{1,0},{2,3},{3,2},{4,5},{5,4},{6,7},{7,6},{8,9},{9,8},{10,11... | collective-permute-start | bytes 884744 | tf_op jit(solution)/shard_map/ppermute | solution.py:38
  19.8 6.7 %collective-permute-start.9 = (bf16[384,384]{1,0:T(8,128)(2,1)S(1)}, bf16[384,384]{1,0:T(8,128)(2,1)S(1)}, u32[]{:S(2)}, u32[]{:S(2)}) collective-permute-start(bf16[384,384]{1,0:T(8,128)(2,1)S(1)} %constant_dynamic-update-slice_fusion.2.refs_8_), channel_id=1, source_target_pairs={{0,8},{4,12},{8,0},{12,4},{16,24},{20,28},{24,16},{28,20},{1,9},{5... | collective-permute-start | bytes 884744 | tf_op jit(solution)/shard_map/ppermute | solution.py:38
  21.5 6.5 %collective-permute-start.5 = (bf16[384,384]{1,0:T(8,128)(2,1)S(1)}, bf16[384,384]{1,0:T(8,128)(2,1)S(1)}, u32[]{:S(2)}, u32[]{:S(2)}) collective-permute-start(bf16[384,384]{1,0:T(8,128)(2,1)S(1)} %collective-permute-done.4.refs_6_), channel_id=1, source_target_pairs={{0,1},{1,0},{2,3},{3,2},{4,5},{5,4},{6,7},{7,6},{8,9},{9,8},{10,11... | collective-permute-start | bytes 884744 | tf_op jit(solution)/shard_map/ppermute | solution.py:38
  21.9 1.4 %copy-start = (bf16[256,3072]{1,0:T(8,128)(2,1)S(1)}, bf16[256,3072]{1,0:T(8,128)(2,1)}, u32[]{:S(2)}) copy-start(bf16[256,3072]{1,0:T(8,128)(2,1)} %refs_4_.1) | copy-start | bytes 4718596
  23.4 21.9 %copy-start.3 = (f32[128]{0:T(128)S(1)}, f32[128]{0:T(128)}, u32[]{:S(2)}) copy-start(f32[128]{0:T(128)} %param.9) | copy-start | bytes 1540
  23.4 21.8 %copy-start.4 = (f32[128]{0:T(128)S(1)}, f32[128]{0:T(128)}, u32[]{:S(2)}) copy-start(f32[128]{0:T(128)} %param.10) | copy-start | bytes 1540
  23.4 10.8 %collective-permute-start.8 = (bf16[384,384]{1,0:T(8,128)(2,1)S(1)}, bf16[384,384]{1,0:T(8,128)(2,1)S(1)}, u32[]{:S(2)}, u32[]{:S(2)}) collective-permute-start(bf16[384,384]{1,0:T(8,128)(2,1)S(1)} %constant_dynamic-update-slice_fusion.2.refs_8_), channel_id=1, source_target_pairs={{0,1},{1,0},{2,3},{3,2},{4,5},{5,4},{6,7},{7,6},{8,9},{9,8},{10,11... | collective-permute-start | bytes 884744 | tf_op jit(solution)/shard_map/ppermute | solution.py:38
  34.2 4.9 %collective-permute-start.10 = (bf16[256,1536]{1,0:T(8,128)(2,1)S(1)}, bf16[256,1536]{1,0:T(8,128)(2,1)S(1)}, u32[]{:S(2)}, u32[]{:S(2)}) collective-permute-start(bf16[256,1536]{1,0:T(8,128)(2,1)S(1)} %collective-permute-done.3.refs_0_), channel_id=1, source_target_pairs={{0,2},{2,0},{1,3},{3,1},{4,6},{6,4},{5,7},{7,5},{8,10},{10,8},{9,1... | collective-permute-start | bytes 2359304 | tf_op jit(solution)/shard_map/ppermute | solution.py:38
  37.2 35.3 %collective-permute-start.21 = (bf16[256,1536]{1,0:T(8,128)(2,1)S(1)}, bf16[256,1536]{1,0:T(8,128)(2,1)S(1)}, u32[]{:S(2)}, u32[]{:S(2)}) collective-permute-start(bf16[256,1536]{1,0:T(8,128)(2,1)S(1)} %constant_dynamic-slice_fusion), channel_id=1, source_target_pairs={{0,2},{2,0},{1,3},{3,1},{4,6},{6,4},{5,7},{7,5},{8,10},{10,8},{9,1... | collective-permute-start | bytes 2359304 | tf_op jit(solution)/shard_map/ppermute | solution.py:38
  37.2 8.1 %collective-permute-start.11 = (bf16[384,384]{1,0:T(8,128)(2,1)S(1)}, bf16[384,384]{1,0:T(8,128)(2,1)S(1)}, u32[]{:S(2)}, u32[]{:S(2)}) collective-permute-start(bf16[384,384]{1,0:T(8,128)(2,1)S(1)} %collective-permute-done.9.refs_10_), channel_id=1, source_target_pairs={{0,1},{1,0},{2,3},{3,2},{4,5},{5,4},{6,7},{7,6},{8,9},{9,8},{10,11... | collective-permute-start | bytes 884744 | tf_op jit(solution)/shard_map/ppermute | solution.py:38
  47.4 4.8 %collective-permute-start.13 = (bf16[256,256]{1,0:T(8,128)(2,1)S(1)}, bf16[256,256]{1,0:T(8,128)(2,1)S(1)}, u32[]{:S(2)}, u32[]{:S(2)}) collective-permute-start(bf16[256,256]{1,0:T(8,128)(2,1)S(1)} %get-tuple-element.23.refs_2_), channel_id=1, source_target_pairs={{0,16},{4,20},{8,24},{12,28},{16,0},{20,4},{24,8},{28,12},{1,17},{... | collective-permute-start | bytes 393224 | tf_op jit(solution)/shard_map/ppermute | solution.py:38
  49.2 11.7 %collective-permute-start.16 = (bf16[256,256]{1,0:T(8,128)(2,1)S(1)}, bf16[256,256]{1,0:T(8,128)(2,1)S(1)}, u32[]{:S(2)}, u32[]{:S(2)}) collective-permute-start(bf16[256,256]{1,0:T(8,128)(2,1)S(1)} %get-tuple-element.24.refs_6_), channel_id=1, source_target_pairs={{0,16},{4,20},{8,24},{12,28},{16,0},{20,4},{24,8},{28,12},{1,17},{... | collective-permute-start | bytes 393224 | tf_op jit(solution)/shard_map/ppermute | solution.py:38
  49.8 12.3 %collective-permute-start.12 = (bf16[256,256]{1,0:T(8,128)(2,1)S(1)}, bf16[256,256]{1,0:T(8,128)(2,1)S(1)}, u32[]{:S(2)}, u32[]{:S(2)}) collective-permute-start(bf16[256,256]{1,0:T(8,128)(2,1)S(1)} %get-tuple-element.23.refs_2_), channel_id=1, source_target_pairs={{0,8},{4,12},{8,0},{12,4},{16,24},{20,28},{24,16},{28,20},{1,9},{5... | collective-permute-start | bytes 393224 | tf_op jit(solution)/shard_map/ppermute | solution.py:38
  51.5 10.6 %collective-permute-start.15 = (bf16[256,256]{1,0:T(8,128)(2,1)S(1)}, bf16[256,256]{1,0:T(8,128)(2,1)S(1)}, u32[]{:S(2)}, u32[]{:S(2)}) collective-permute-start(bf16[256,256]{1,0:T(8,128)(2,1)S(1)} %get-tuple-element.24.refs_6_), channel_id=1, source_target_pairs={{0,8},{4,12},{8,0},{12,4},{16,24},{20,28},{24,16},{28,20},{1,9},{5... | collective-permute-start | bytes 393224 | tf_op jit(solution)/shard_map/ppermute | solution.py:38
  52.2 11.5 %collective-permute-start.14 = (bf16[256,256]{1,0:T(8,128)(2,1)S(1)}, bf16[256,256]{1,0:T(8,128)(2,1)S(1)}, u32[]{:S(2)}, u32[]{:S(2)}) collective-permute-start(bf16[256,256]{1,0:T(8,128)(2,1)S(1)} %collective-permute-done.13.refs_4_), channel_id=1, source_target_pairs={{0,8},{4,12},{8,0},{12,4},{16,24},{20,28},{24,16},{28,20},{1,9},{5... | collective-permute-start | bytes 393224 | tf_op jit(solution)/shard_map/ppermute | solution.py:38
  60.9 5.3 %collective-permute-start.17 = (bf16[256,256]{1,0:T(8,128)(2,1)S(1)}, bf16[256,256]{1,0:T(8,128)(2,1)S(1)}, u32[]{:S(2)}, u32[]{:S(2)}) collective-permute-start(bf16[256,256]{1,0:T(8,128)(2,1)S(1)} %collective-permute-done.16.refs_8_), channel_id=1, source_target_pairs={{0,8},{4,12},{8,0},{12,4},{16,24},{20,28},{24,16},{28,20},{1,9},{5... | collective-permute-start | bytes 393224 | tf_op jit(solution)/shard_map/ppermute | solution.py:38
  68.4 4.1 %collective-permute-start.18 = (bf16[256,128]{1,0:T(8,128)(2,1)S(1)}, bf16[256,128]{1,0:T(8,128)(2,1)S(1)}, u32[]{:S(2)}, u32[]{:S(2)}) collective-permute-start(bf16[256,128]{1,0:T(8,128)(2,1)S(1)} %get-tuple-element.26), channel_id=1, source_target_pairs={{0,4},{2,6},{4,0},{6,2},{8,12},{10,14},{12,8},{14,10},{16,20},{18,... | collective-permute-start | bytes 196616 | tf_op jit(solution)/shard_map/ppermute | solution.py:38
  69.7 3.2 %collective-permute-start.19 = (bf16[256,128]{1,0:T(8,128)(2,1)S(1)}, bf16[256,128]{1,0:T(8,128)(2,1)S(1)}, u32[]{:S(2)}, u32[]{:S(2)}) collective-permute-start(bf16[256,128]{1,0:T(8,128)(2,1)S(1)} %get-tuple-element.25.refs_0_), channel_id=1, source_target_pairs={{0,2},{2,0},{4,6},{6,4},{8,10},{10,8},{12,14},{14,12},{16,18},{18,... | collective-permute-start | bytes 196616 | tf_op jit(solution)/shard_map/ppermute | solution.py:38
  72.0 3.9 %collective-permute-start.20 = (bf16[256,128]{1,0:T(8,128)(2,1)S(1)}, bf16[256,128]{1,0:T(8,128)(2,1)S(1)}, u32[]{:S(2)}, u32[]{:S(2)}) collective-permute-start(bf16[256,128]{1,0:T(8,128)(2,1)S(1)} %get-tuple-element.26), channel_id=1, source_target_pairs={{0,6},{2,4},{4,2},{6,0},{8,14},{10,12},{12,10},{14,8},{16,22},{18,... | collective-permute-start | bytes 196616 | tf_op jit(solution)/shard_map/ppermute | solution.py:38
